TPU v7x, 128 devices: a whole 4x4x4 slice. The times are simulated.
128 devices in a mesh: blk: 8 (over z, y_lo), group: 16 (over x, y_hi, core).
Axes of the slice: x: 4, y: 4 (y_hi: 2, y_lo: 2; y = y_hi * 2 + y_lo), z: 4, core: 2. Of those that a mesh axis runs over, the one named last changes fastest.
Arguments:
- img_feat: bfloat16 [16384, 1152], P(('blk', 'group')), may hold values from -150 to 150
- txt_feat: bfloat16 [16384, 1152], P(('blk', 'group')), may hold values from -150 to 150
- w_img: bfloat16 [1152, 1152], replicated, may hold values from -1 to 2
- w_txt: bfloat16 [1152, 1152], replicated, may hold values from -1 to 2
- logit_scale_log: float32 [1], replicated, may hold values from 2.3 to 4.8
- bias: float32 [1], replicated, may hold values from -12 to -6
Outputs:
- grad_img_feat: bfloat16 [16384, 1152], P(('blk', 'group'))
- grad_txt_feat: bfloat16 [16384, 1152], P(('blk', 'group'))
- grad_w_img: float32 [1152, 1152], P(('blk', 'group'))
- grad_w_txt: float32 [1152, 1152], P(('blk', 'group'))
All inputs are finite; a program needn't handle non-finite values.
Results may differ from a plain program's by a relative error of at most 0.025.
Values may be sent and summed in bfloat16 or wider, within the bound.
A program may use at most 128 MiB of HBM per device.

v0:
```python
import jax
import jax.numpy as jnp
from jax import lax
from jax.sharding import PartitionSpec as P


def passed_along(value, axis, steps):
    count = lax.axis_size(axis)
    pairs = [(source, (source + steps) % count) for source in range(count)]
    return lax.ppermute(value, axis, pairs)


def unit_rows(projected):
    inverse = lax.rsqrt(jnp.sum(projected * projected, axis=1, keepdims=True) + 1e-06)
    return (projected * inverse, inverse)


def through_norm(unit, inverse, upstream):
    return inverse * (upstream - unit * jnp.sum(unit * upstream, axis=1, keepdims=True))


def shift_texts(pieces):
    moved = (passed_along(pieces[0], "blk", 1),)
    return moved


def shift_partials(partials):
    moved = (passed_along(partials[0].astype(jnp.bfloat16), "blk", 1).astype(jnp.float32),)
    return moved


def body(img_feat, txt_feat, w_img, w_txt, logit_scale_log, bias):
    scale_factor = jnp.exp(logit_scale_log[0])
    logit_bias_value = bias[0]
    unit_img, inverse_img = unit_rows(jnp.dot(img_feat, w_img, preferred_element_type=jnp.float32))
    unit_txt, inverse_txt = unit_rows(jnp.dot(txt_feat, w_txt, preferred_element_type=jnp.float32))
    emb_img = unit_img.astype(jnp.bfloat16)
    emb_txt = unit_txt.astype(jnp.bfloat16)
    block_img = lax.all_gather(emb_img, "group", axis=0, tiled=True)
    local_rows = emb_txt.shape[0]
    width = emb_txt.shape[1]
    block_rows = block_img.shape[0]
    loop_size = lax.axis_size("blk")
    blk_index = lax.axis_index("blk")
    group_index = lax.axis_index("group")
    image_ids = blk_index * block_rows + jnp.arange(block_rows, dtype=jnp.int32)
    spans = ((0, local_rows, 1),)
    start_pieces = tuple((emb_txt for start_row, stop_row, heading in spans))
    start_partials = tuple(
        (
            jnp.zeros((stop_row - start_row, width), jnp.float32)
            for start_row, stop_row, heading in spans
        )
    )

    def one_step(step_index, state):
        pieces, partials, image_grad = state
        anchors = [
            (blk_index - heading * step_index) % loop_size for start_row, stop_row, heading in spans
        ]
        text_ids = jnp.concatenate(
            [
                anchor * block_rows
                + group_index * local_rows
                + start_row
                + jnp.arange(stop_row - start_row, dtype=jnp.int32)
                for anchor, (start_row, stop_row, heading) in zip(anchors, spans)
            ]
        )
        texts_now = pieces[0]
        similarity_grid = lax.dot_general(
            block_img, texts_now, (((1,), (1,)), ((), ())), preferred_element_type=jnp.float32
        )
        pair_scores = scale_factor * similarity_grid + logit_bias_value
        match_signs = jnp.where(image_ids[:, None] == text_ids[None, :], 1.0, -1.0).astype(
            jnp.float32
        )
        weight_matrices = (
            -match_signs * jax.nn.sigmoid(-match_signs * pair_scores) * scale_factor
        ).astype(jnp.bfloat16)
        image_grad = image_grad + jnp.dot(
            weight_matrices, texts_now, preferred_element_type=jnp.float32
        )
        text_grad = lax.dot_general(
            weight_matrices, block_img, (((0,), (0,)), ((), ())), preferred_element_type=jnp.float32
        )
        partials = shift_partials(
            tuple(
                (
                    partial_value + text_grad
                    for partial_value, (start_row, stop_row, heading) in zip(partials, spans)
                )
            )
        )
        return (shift_texts(pieces), partials, image_grad)

    image_start = jnp.zeros((block_rows, width), jnp.float32)
    final_pieces, final_partials, image_grad = lax.fori_loop(
        0, loop_size, one_step, (start_pieces, start_partials, image_start)
    )
    grad_emb_txt = final_partials[0]
    grad_emb_img = lax.psum_scatter(
        image_grad.astype(jnp.bfloat16), "group", scatter_dimension=0, tiled=True
    ).astype(jnp.float32)
    grad_proj_img = through_norm(unit_img, inverse_img, grad_emb_img).astype(jnp.bfloat16)
    grad_proj_txt = through_norm(unit_txt, inverse_txt, grad_emb_txt).astype(jnp.bfloat16)
    grad_img_feat = lax.dot_general(
        grad_proj_img, w_img, (((1,), (1,)), ((), ())), preferred_element_type=jnp.float32
    ).astype(jnp.bfloat16)
    grad_txt_feat = lax.dot_general(
        grad_proj_txt, w_txt, (((1,), (1,)), ((), ())), preferred_element_type=jnp.float32
    ).astype(jnp.bfloat16)
    img_term = lax.dot_general(
        img_feat, grad_proj_img, (((0,), (0,)), ((), ())), preferred_element_type=jnp.float32
    )
    txt_term = lax.dot_general(
        txt_feat, grad_proj_txt, (((0,), (0,)), ((), ())), preferred_element_type=jnp.float32
    )
    both_grads = lax.psum_scatter(
        jnp.concatenate([img_term, txt_term], axis=1),
        ("blk", "group"),
        scatter_dimension=0,
        tiled=True,
    )
    grad_w_img = both_grads[:, :width]
    grad_w_txt = both_grads[:, width:]
    return (grad_img_feat, grad_txt_feat, grad_w_img, grad_w_txt)


def solution(mesh):
    placed = (P(("blk", "group"), None), P(("blk", "group"), None), P(), P(), P(), P())
    return jax.shard_map(
        body,
        mesh=mesh,
        in_specs=placed,
        out_specs=(
            P(("blk", "group"), None),
            P(("blk", "group"), None),
            P(("blk", "group"), None),
            P(("blk", "group"), None),
        ),
        check_vma=False,
    )
```

profile of v0, /device:TPU:1, one launch (start us, length us, event | category | flops | bytes accessed | tf_op | source)
XLA Modules:
  0.0 514.1 jit_solution(11114435810228768485)
XLA Ops:
  14.7 58.5 %all-gather.2.cloned.1.call-done = bf16[2048,1152]{1,0:T(8,128)(2,1)} async-done(((bf16[128,1152]{1,0:T(8,128)(2,1)}), bf16[2048,1152]{1,0:T(8,128)(2,1)}) %all-gather.2.cloned.1.call-update) | async-done | bytes 4718608 | tf_op jit(solution)/shard_map/all_gather | solution.py:39
  73.2 156.0 %while.20 = (s32[]{:T(128)}, bf16[128,1152]{1,0:T(8,128)(2,1)}, f32[128,1152]{1,0:T(8,128)}, f32[2048,1152]{1,0:T(8,128)}, s32[]{:T(128)}, /*index=5*/s32[]{:T(1...) while((s32[]{:T(128)}, bf16[128,1152]{1,0:T(8,128)(2,1)}, ...), condition=%wide.region_3.4_spmd.clone, body=%wide.region_2.3_spmd.clone.sunk | while | flops 1820395648 | bytes 51725776 | solution.py:98
  74.6 5.2 %fusion.48 = bf16[2048,128]{1,0:T(8,128)(2,1)S(1)} fusion(bf16[2048,1152]{1,0:T(8,128)(2,1)} %get-tuple-element.420, bf16[128,1152]{1,0:T(8,128)(2,1)S(1)} %copy.21, f32[]{:T(128)} %get-tuple-element.421, f32[]{:T(128)} %get-tuple-element.419, s32[128]{0:T(128)S(1)} %iota_add_fusion.4, s32[2048]{0:T(1024)S(1)} %iota_add_fusion.5), kind=kOutput, calls=%fused_computation.12.clone.1 | convolution fusion | flops 607125504 | bytes 5546504 | tf_op jit(solution)/shard_map/while/body/eval_jaxpr/dot_general | solution.py:71
  83.6 5.0 convolution_add_fusion.3
  93.7 5.2 %fusion.48 = bf16[2048,128]{1,0:T(8,128)(2,1)S(1)} fusion(bf16[2048,1152]{1,0:T(8,128)(2,1)} %get-tuple-element.420, bf16[128,1152]{1,0:T(8,128)(2,1)S(1)} %copy.21, f32[]{:T(128)} %get-tuple-element.421, f32[]{:T(128)} %get-tuple-element.419, s32[128]{0:T(128)S(1)} %iota_add_fusion.4, s32[2048]{0:T(1024)S(1)} %iota_add_fusion.5), kind=kOutput, calls=%fused_computation.12.clone.1 | convolution fusion | flops 607125504 | bytes 5546504 | tf_op jit(solution)/shard_map/while/body/eval_jaxpr/dot_general | solution.py:71
  101.8 8.7 %convolution_add_fusion.3 = f32[2048,1152]{1,0:T(8,128)} fusion(bf16[2048,128]{1,0:T(8,128)(2,1)S(1)} %fusion.48, bf16[128,1152]{1,0:T(8,128)(2,1)S(1)} %copy.21, f32[2048,1152]{1,0:T(8,128)} %get-tuple-element.401, pred[]{:T(512)S(6)} %compare.4), kind=kOutput, calls=%fused_computation.1.clone.1 | convolution fusion | flops 608698368 | bytes 19693568 | tf_op jit(solution)/shard_map/while/body/eval_jaxpr/dot_general | solution.py:81
  113.7 5.2 %fusion.48 = bf16[2048,128]{1,0:T(8,128)(2,1)S(1)} fusion(bf16[2048,1152]{1,0:T(8,128)(2,1)} %get-tuple-element.420, bf16[128,1152]{1,0:T(8,128)(2,1)S(1)} %copy.21, f32[]{:T(128)} %get-tuple-element.421, f32[]{:T(128)} %get-tuple-element.419, s32[128]{0:T(128)S(1)} %iota_add_fusion.4, s32[2048]{0:T(1024)S(1)} %iota_add_fusion.5), kind=kOutput, calls=%fused_computation.12.clone.1 | convolution fusion | flops 607125504 | bytes 5546504 | tf_op jit(solution)/shard_map/while/body/eval_jaxpr/dot_general | solution.py:71
  121.8 8.7 %convolution_add_fusion.3 = f32[2048,1152]{1,0:T(8,128)} fusion(bf16[2048,128]{1,0:T(8,128)(2,1)S(1)} %fusion.48, bf16[128,1152]{1,0:T(8,128)(2,1)S(1)} %copy.21, f32[2048,1152]{1,0:T(8,128)} %get-tuple-element.401, pred[]{:T(512)S(6)} %compare.4), kind=kOutput, calls=%fused_computation.1.clone.1 | convolution fusion | flops 608698368 | bytes 19693568 | tf_op jit(solution)/shard_map/while/body/eval_jaxpr/dot_general | solution.py:81
  133.3 5.2 %fusion.48 = bf16[2048,128]{1,0:T(8,128)(2,1)S(1)} fusion(bf16[2048,1152]{1,0:T(8,128)(2,1)} %get-tuple-element.420, bf16[128,1152]{1,0:T(8,128)(2,1)S(1)} %copy.21, f32[]{:T(128)} %get-tuple-element.421, f32[]{:T(128)} %get-tuple-element.419, s32[128]{0:T(128)S(1)} %iota_add_fusion.4, s32[2048]{0:T(1024)S(1)} %iota_add_fusion.5), kind=kOutput, calls=%fused_computation.12.clone.1 | convolution fusion | flops 607125504 | bytes 5546504 | tf_op jit(solution)/shard_map/while/body/eval_jaxpr/dot_general | solution.py:71
  141.4 8.7 %convolution_add_fusion.3 = f32[2048,1152]{1,0:T(8,128)} fusion(bf16[2048,128]{1,0:T(8,128)(2,1)S(1)} %fusion.48, bf16[128,1152]{1,0:T(8,128)(2,1)S(1)} %copy.21, f32[2048,1152]{1,0:T(8,128)} %get-tuple-element.401, pred[]{:T(512)S(6)} %compare.4), kind=kOutput, calls=%fused_computation.1.clone.1 | convolution fusion | flops 608698368 | bytes 19693568 | tf_op jit(solution)/shard_map/while/body/eval_jaxpr/dot_general | solution.py:81
  152.0 5.2 %fusion.48 = bf16[2048,128]{1,0:T(8,128)(2,1)S(1)} fusion(bf16[2048,1152]{1,0:T(8,128)(2,1)} %get-tuple-element.420, bf16[128,1152]{1,0:T(8,128)(2,1)S(1)} %copy.21, f32[]{:T(128)} %get-tuple-element.421, f32[]{:T(128)} %get-tuple-element.419, s32[128]{0:T(128)S(1)} %iota_add_fusion.4, s32[2048]{0:T(1024)S(1)} %iota_add_fusion.5), kind=kOutput, calls=%fused_computation.12.clone.1 | convolution fusion | flops 607125504 | bytes 5546504 | tf_op jit(solution)/shard_map/while/body/eval_jaxpr/dot_general | solution.py:71
  161.3 8.7 %convolution_add_fusion.3 = f32[2048,1152]{1,0:T(8,128)} fusion(bf16[2048,128]{1,0:T(8,128)(2,1)S(1)} %fusion.48, bf16[128,1152]{1,0:T(8,128)(2,1)S(1)} %copy.21, f32[2048,1152]{1,0:T(8,128)} %get-tuple-element.401, pred[]{:T(512)S(6)} %compare.4), kind=kOutput, calls=%fused_computation.1.clone.1 | convolution fusion | flops 608698368 | bytes 19693568 | tf_op jit(solution)/shard_map/while/body/eval_jaxpr/dot_general | solution.py:81
  171.9 5.2 %fusion.48 = bf16[2048,128]{1,0:T(8,128)(2,1)S(1)} fusion(bf16[2048,1152]{1,0:T(8,128)(2,1)} %get-tuple-element.420, bf16[128,1152]{1,0:T(8,128)(2,1)S(1)} %copy.21, f32[]{:T(128)} %get-tuple-element.421, f32[]{:T(128)} %get-tuple-element.419, s32[128]{0:T(128)S(1)} %iota_add_fusion.4, s32[2048]{0:T(1024)S(1)} %iota_add_fusion.5), kind=kOutput, calls=%fused_computation.12.clone.1 | convolution fusion | flops 607125504 | bytes 5546504 | tf_op jit(solution)/shard_map/while/body/eval_jaxpr/dot_general | solution.py:71
  180.0 8.7 %convolution_add_fusion.3 = f32[2048,1152]{1,0:T(8,128)} fusion(bf16[2048,128]{1,0:T(8,128)(2,1)S(1)} %fusion.48, bf16[128,1152]{1,0:T(8,128)(2,1)S(1)} %copy.21, f32[2048,1152]{1,0:T(8,128)} %get-tuple-element.401, pred[]{:T(512)S(6)} %compare.4), kind=kOutput, calls=%fused_computation.1.clone.1 | convolution fusion | flops 608698368 | bytes 19693568 | tf_op jit(solution)/shard_map/while/body/eval_jaxpr/dot_general | solution.py:81
  191.9 5.2 %fusion.48 = bf16[2048,128]{1,0:T(8,128)(2,1)S(1)} fusion(bf16[2048,1152]{1,0:T(8,128)(2,1)} %get-tuple-element.420, bf16[128,1152]{1,0:T(8,128)(2,1)S(1)} %copy.21, f32[]{:T(128)} %get-tuple-element.421, f32[]{:T(128)} %get-tuple-element.419, s32[128]{0:T(128)S(1)} %iota_add_fusion.4, s32[2048]{0:T(1024)S(1)} %iota_add_fusion.5), kind=kOutput, calls=%fused_computation.12.clone.1 | convolution fusion | flops 607125504 | bytes 5546504 | tf_op jit(solution)/shard_map/while/body/eval_jaxpr/dot_general | solution.py:71
  200.0 8.7 %convolution_add_fusion.3 = f32[2048,1152]{1,0:T(8,128)} fusion(bf16[2048,128]{1,0:T(8,128)(2,1)S(1)} %fusion.48, bf16[128,1152]{1,0:T(8,128)(2,1)S(1)} %copy.21, f32[2048,1152]{1,0:T(8,128)} %get-tuple-element.401, pred[]{:T(512)S(6)} %compare.4), kind=kOutput, calls=%fused_computation.1.clone.1 | convolution fusion | flops 608698368 | bytes 19693568 | tf_op jit(solution)/shard_map/while/body/eval_jaxpr/dot_general | solution.py:81
  211.5 5.2 %fusion.48 = bf16[2048,128]{1,0:T(8,128)(2,1)S(1)} fusion(bf16[2048,1152]{1,0:T(8,128)(2,1)} %get-tuple-element.420, bf16[128,1152]{1,0:T(8,128)(2,1)S(1)} %copy.21, f32[]{:T(128)} %get-tuple-element.421, f32[]{:T(128)} %get-tuple-element.419, s32[128]{0:T(128)S(1)} %iota_add_fusion.4, s32[2048]{0:T(1024)S(1)} %iota_add_fusion.5), kind=kOutput, calls=%fused_computation.12.clone.1 | convolution fusion | flops 607125504 | bytes 5546504 | tf_op jit(solution)/shard_map/while/body/eval_jaxpr/dot_general | solution.py:71
  219.6 8.7 %convolution_add_fusion.3 = f32[2048,1152]{1,0:T(8,128)} fusion(bf16[2048,128]{1,0:T(8,128)(2,1)S(1)} %fusion.48, bf16[128,1152]{1,0:T(8,128)(2,1)S(1)} %copy.21, f32[2048,1152]{1,0:T(8,128)} %get-tuple-element.401, pred[]{:T(512)S(6)} %compare.4), kind=kOutput, calls=%fused_computation.1.clone.1 | convolution fusion | flops 608698368 | bytes 19693568 | tf_op jit(solution)/shard_map/while/body/eval_jaxpr/dot_general | solution.py:81
  229.2 6.3 %convert_element_type.56 = bf16[2048,1152]{1,0:T(8,128)(2,1)} convert(f32[2048,1152]{1,0:T(8,128)} %get-tuple-element.250) | non-fusion elementwise | flops 2359296 | bytes 14155776 | tf_op jit(solution)/shard_map/convert_element_type | solution.py:103
  239.0 4.3 convolution_bitcast_fusion
  243.3 77.1 %reduce-scatter.3.cloned.1.call-done = bf16[128,1152]{1,0:T(8,128)(2,1)} async-done(((bf16[2048,1152]{1,0:T(8,128)(2,1)}), bf16[128,1152]{1,0:T(8,128)(2,1)}) %reduce-scatter.3.cloned.1.call-update) | async-done | bytes 294928 | tf_op jit(solution)/shard_map/reduce_scatter | solution.py:102
  323.5 4.1 convolution_bitcast_fusion.1
  327.6 8.8 %pad_maximum_fusion = f32[1152,2304]{0,1:T(8,128)} fusion(f32[1152,1152]{0,1:T(8,128)} %convolution_bitcast_fusion, f32[1152,1152]{0,1:T(8,128)} %convolution_bitcast_fusion.1), kind=kLoop, calls=%fused_computation.16 | loop fusion | flops 2654208 | bytes 21233664 | tf_op jit(solution)/shard_map/concatenate | solution.py:120
  341.5 160.5 %all-reduce.3.cloned.1.call-done = f32[1152,2304]{0,1:T(8,128)} async-done(((f32[1152,2304]{0,1:T(8,128)}), f32[1152,2304]{0,1:T(8,128)}) %all-reduce.3.cloned.1.call-update) | async-done | bytes 10616848
  (167 shorter events, 71.8 us)
Async XLA Ops:
  7.2 66.0 %all-gather.2.cloned.1.call-start = ((), (), s32[]{:S(2)}) async-start(), calls=%async_computation.1 | async-start | bytes 5013504 | tf_op jit(solution)/shard_map/all_gather | solution.py:39
  11.6 308.9 %reduce-scatter.3.cloned.1.call-start = ((), (), s32[]{:S(2)}) async-start(), calls=%async_computation.2 | async-start | bytes 5013504 | tf_op jit(solution)/shard_map/reduce_scatter | solution.py:102
  74.3 18.4 %collective-permute-start = (bf16[128,1152]{1,0:T(8,128)(2,1)S(1)}, bf16[128,1152]{1,0:T(8,128)(2,1)}, u32[]{:S(2)}, u32[]{:S(2)}) collective-permute-start(bf16[128,1152]{1,0:T(8,128)(2,1)S(1)} %copy.21), channel_id=1, source_target_pairs={{0,16},{16,32},{32,48},{48,64},{64,80},{80,96},{96,112},{112,0},{1... | collective-permute-start | bytes 884744 | tf_op jit(solution)/shard_map/while/body/eval_jaxpr/ppermute | solution.py:10
  81.4 10.4 %collective-permute-start.1 = (bf16[128,1152]{1,0:T(8,128)(2,1)}, bf16[128,1152]{1,0:T(8,128)(2,1)S(1)}, u32[]{:S(2)}, u32[]{:S(2)}) collective-permute-start(bf16[128,1152]{1,0:T(8,128)(2,1)} %fusion.49), channel_id=1, source_target_pairs={{0,16},{16,32},{32,48},{48,64},{64,80},{80,96},{96,112},{112,0},{1... | collective-permute-start | bytes 884744 | tf_op jit(solution)/shard_map/while/body/eval_jaxpr/ppermute | solution.py:10
  93.7 17.7 %collective-permute-start = (bf16[128,1152]{1,0:T(8,128)(2,1)S(1)}, bf16[128,1152]{1,0:T(8,128)(2,1)}, u32[]{:S(2)}, u32[]{:S(2)}) collective-permute-start(bf16[128,1152]{1,0:T(8,128)(2,1)S(1)} %copy.21), channel_id=1, source_target_pairs={{0,16},{16,32},{32,48},{48,64},{64,80},{80,96},{96,112},{112,0},{1... | collective-permute-start | bytes 884744 | tf_op jit(solution)/shard_map/while/body/eval_jaxpr/ppermute | solution.py:10
  100.6 9.9 %collective-permute-start.1 = (bf16[128,1152]{1,0:T(8,128)(2,1)}, bf16[128,1152]{1,0:T(8,128)(2,1)S(1)}, u32[]{:S(2)}, u32[]{:S(2)}) collective-permute-start(bf16[128,1152]{1,0:T(8,128)(2,1)} %fusion.49), channel_id=1, source_target_pairs={{0,16},{16,32},{32,48},{48,64},{64,80},{80,96},{96,112},{112,0},{1... | collective-permute-start | bytes 884744 | tf_op jit(solution)/shard_map/while/body/eval_jaxpr/ppermute | solution.py:10
  111.4 7.5 %slice-start = ((s8[4718592]{0:T(1024)(128)(4,1)}), s8[524288]{0:T(1024)(128)(4,1)S(1)}, s32[]{:S(2)}) async-start(s8[4718592]{0:T(1024)(128)(4,1)} %bitcast.38), calls=%async_computation.4 | async-start | bytes 1048576 | tf_op jit(solution)/shard_map/while
  112.4 18.9 %collective-permute-start = (bf16[128,1152]{1,0:T(8,128)(2,1)S(1)}, bf16[128,1152]{1,0:T(8,128)(2,1)}, u32[]{:S(2)}, u32[]{:S(2)}) collective-permute-start(bf16[128,1152]{1,0:T(8,128)(2,1)S(1)} %copy.21), channel_id=1, source_target_pairs={{0,16},{16,32},{32,48},{48,64},{64,80},{80,96},{96,112},{112,0},{1... | collective-permute-start | bytes 884744 | tf_op jit(solution)/shard_map/while/body/eval_jaxpr/ppermute | solution.py:10
  120.5 9.9 %collective-permute-start.1 = (bf16[128,1152]{1,0:T(8,128)(2,1)}, bf16[128,1152]{1,0:T(8,128)(2,1)S(1)}, u32[]{:S(2)}, u32[]{:S(2)}) collective-permute-start(bf16[128,1152]{1,0:T(8,128)(2,1)} %fusion.49), channel_id=1, source_target_pairs={{0,16},{16,32},{32,48},{48,64},{64,80},{80,96},{96,112},{112,0},{1... | collective-permute-start | bytes 884744 | tf_op jit(solution)/shard_map/while/body/eval_jaxpr/ppermute | solution.py:10
  131.3 7.2 %slice-start = ((s8[4718592]{0:T(1024)(128)(4,1)}), s8[524288]{0:T(1024)(128)(4,1)S(1)}, s32[]{:S(2)}) async-start(s8[4718592]{0:T(1024)(128)(4,1)} %bitcast.38), calls=%async_computation.4 | async-start | bytes 1048576 | tf_op jit(solution)/shard_map/while
  132.4 18.6 %collective-permute-start = (bf16[128,1152]{1,0:T(8,128)(2,1)S(1)}, bf16[128,1152]{1,0:T(8,128)(2,1)}, u32[]{:S(2)}, u32[]{:S(2)}) collective-permute-start(bf16[128,1152]{1,0:T(8,128)(2,1)S(1)} %copy.21), channel_id=1, source_target_pairs={{0,16},{16,32},{32,48},{48,64},{64,80},{80,96},{96,112},{112,0},{1... | collective-permute-start | bytes 884744 | tf_op jit(solution)/shard_map/while/body/eval_jaxpr/ppermute | solution.py:10
  140.2 9.9 %collective-permute-start.1 = (bf16[128,1152]{1,0:T(8,128)(2,1)}, bf16[128,1152]{1,0:T(8,128)(2,1)S(1)}, u32[]{:S(2)}, u32[]{:S(2)}) collective-permute-start(bf16[128,1152]{1,0:T(8,128)(2,1)} %fusion.49), channel_id=1, source_target_pairs={{0,16},{16,32},{32,48},{48,64},{64,80},{80,96},{96,112},{112,0},{1... | collective-permute-start | bytes 884744 | tf_op jit(solution)/shard_map/while/body/eval_jaxpr/ppermute | solution.py:10
  152.0 18.9 %collective-permute-start = (bf16[128,1152]{1,0:T(8,128)(2,1)S(1)}, bf16[128,1152]{1,0:T(8,128)(2,1)}, u32[]{:S(2)}, u32[]{:S(2)}) collective-permute-start(bf16[128,1152]{1,0:T(8,128)(2,1)S(1)} %copy.21), channel_id=1, source_target_pairs={{0,16},{16,32},{32,48},{48,64},{64,80},{80,96},{96,112},{112,0},{1... | collective-permute-start | bytes 884744 | tf_op jit(solution)/shard_map/while/body/eval_jaxpr/ppermute | solution.py:10
  158.9 11.1 %collective-permute-start.1 = (bf16[128,1152]{1,0:T(8,128)(2,1)}, bf16[128,1152]{1,0:T(8,128)(2,1)S(1)}, u32[]{:S(2)}, u32[]{:S(2)}) collective-permute-start(bf16[128,1152]{1,0:T(8,128)(2,1)} %fusion.49), channel_id=1, source_target_pairs={{0,16},{16,32},{32,48},{48,64},{64,80},{80,96},{96,112},{112,0},{1... | collective-permute-start | bytes 884744 | tf_op jit(solution)/shard_map/while/body/eval_jaxpr/ppermute | solution.py:10
  171.9 17.7 %collective-permute-start = (bf16[128,1152]{1,0:T(8,128)(2,1)S(1)}, bf16[128,1152]{1,0:T(8,128)(2,1)}, u32[]{:S(2)}, u32[]{:S(2)}) collective-permute-start(bf16[128,1152]{1,0:T(8,128)(2,1)S(1)} %copy.21), channel_id=1, source_target_pairs={{0,16},{16,32},{32,48},{48,64},{64,80},{80,96},{96,112},{112,0},{1... | collective-permute-start | bytes 884744 | tf_op jit(solution)/shard_map/while/body/eval_jaxpr/ppermute | solution.py:10
  178.8 9.9 %collective-permute-start.1 = (bf16[128,1152]{1,0:T(8,128)(2,1)}, bf16[128,1152]{1,0:T(8,128)(2,1)S(1)}, u32[]{:S(2)}, u32[]{:S(2)}) collective-permute-start(bf16[128,1152]{1,0:T(8,128)(2,1)} %fusion.49), channel_id=1, source_target_pairs={{0,16},{16,32},{32,48},{48,64},{64,80},{80,96},{96,112},{112,0},{1... | collective-permute-start | bytes 884744 | tf_op jit(solution)/shard_map/while/body/eval_jaxpr/ppermute | solution.py:10
  189.6 7.5 %slice-start = ((s8[4718592]{0:T(1024)(128)(4,1)}), s8[524288]{0:T(1024)(128)(4,1)S(1)}, s32[]{:S(2)}) async-start(s8[4718592]{0:T(1024)(128)(4,1)} %bitcast.38), calls=%async_computation.4 | async-start | bytes 1048576 | tf_op jit(solution)/shard_map/while
  190.6 18.9 %collective-permute-start = (bf16[128,1152]{1,0:T(8,128)(2,1)S(1)}, bf16[128,1152]{1,0:T(8,128)(2,1)}, u32[]{:S(2)}, u32[]{:S(2)}) collective-permute-start(bf16[128,1152]{1,0:T(8,128)(2,1)S(1)} %copy.21), channel_id=1, source_target_pairs={{0,16},{16,32},{32,48},{48,64},{64,80},{80,96},{96,112},{112,0},{1... | collective-permute-start | bytes 884744 | tf_op jit(solution)/shard_map/while/body/eval_jaxpr/ppermute | solution.py:10
  198.7 9.9 %collective-permute-start.1 = (bf16[128,1152]{1,0:T(8,128)(2,1)}, bf16[128,1152]{1,0:T(8,128)(2,1)S(1)}, u32[]{:S(2)}, u32[]{:S(2)}) collective-permute-start(bf16[128,1152]{1,0:T(8,128)(2,1)} %fusion.49), channel_id=1, source_target_pairs={{0,16},{16,32},{32,48},{48,64},{64,80},{80,96},{96,112},{112,0},{1... | collective-permute-start | bytes 884744 | tf_op jit(solution)/shard_map/while/body/eval_jaxpr/ppermute | solution.py:10
  209.5 7.2 %slice-start = ((s8[4718592]{0:T(1024)(128)(4,1)}), s8[524288]{0:T(1024)(128)(4,1)S(1)}, s32[]{:S(2)}) async-start(s8[4718592]{0:T(1024)(128)(4,1)} %bitcast.38), calls=%async_computation.4 | async-start | bytes 1048576 | tf_op jit(solution)/shard_map/while
  210.6 18.6 %collective-permute-start = (bf16[128,1152]{1,0:T(8,128)(2,1)S(1)}, bf16[128,1152]{1,0:T(8,128)(2,1)}, u32[]{:S(2)}, u32[]{:S(2)}) collective-permute-start(bf16[128,1152]{1,0:T(8,128)(2,1)S(1)} %copy.21), channel_id=1, source_target_pairs={{0,16},{16,32},{32,48},{48,64},{64,80},{80,96},{96,112},{112,0},{1... | collective-permute-start | bytes 884744 | tf_op jit(solution)/shard_map/while/body/eval_jaxpr/ppermute | solution.py:10
  218.4 9.9 %collective-permute-start.1 = (bf16[128,1152]{1,0:T(8,128)(2,1)}, bf16[128,1152]{1,0:T(8,128)(2,1)S(1)}, u32[]{:S(2)}, u32[]{:S(2)}) collective-permute-start(bf16[128,1152]{1,0:T(8,128)(2,1)} %fusion.49), channel_id=1, source_target_pairs={{0,16},{16,32},{32,48},{48,64},{64,80},{80,96},{96,112},{112,0},{1... | collective-permute-start | bytes 884744 | tf_op jit(solution)/shard_map/while/body/eval_jaxpr/ppermute | solution.py:10
  235.5 266.5 %all-reduce.3.cloned.1.call-start = ((), (), s32[]{:S(2)}) async-start(), calls=%async_computation.3 | async-start | bytes 21233664
  239.0 81.4 %copy-start.4 = (f32[128,1152]{1,0:T(8,128)S(1)}, f32[128,1152]{1,0:T(8,128)}, u32[]{:S(2)}) copy-start(f32[128,1152]{1,0:T(8,128)} %copy-done.3) | copy-start | bytes 1769476
  (27 other events, 124.4 us)
Sparse Core Ops, SparseCore 0:
  11.7 61.4 all-gather.1
  235.6 84.7 reduce-scatter.2
  336.6 165.3 all-reduce.2
where the time goes:
time: 515 us; the launch traced here: 514 us
  waiting for transfers between devices  299 us (58%)
  matrix products  137 us (27%)
  other arithmetic  28.5 us (6%)
  local copies, waits for them, and re-layouts  17.1 us (3%)
  starting transfers between devices  16.7 us (3%)
  between operations  14.6 us (3%)
    unnamed x4, waiting for transfers between devices  161 us
    reduce_scatter x1, waiting for transfers between devices, body(): lax.psum_scatter(image_grad.astype(jnp.bfloat16), 'group', scatter_dimens...  77.1 us
    dot_general x8, matrix products, one_step(): jnp.dot(weight_matrices, texts_now, preferred_element_type=jnp.float32)  66.1 us
    all_gather x1, waiting for transfers between devices, body(): block_img = lax.all_gather(emb_img, 'group', axis=0, tiled=True)  58.5 us
    dot_general x8, matrix products, one_step(): lax.dot_general(block_img, texts_now, (((1,), (1,)), ((), ())), preferred...  41.5 us
    ppermute x16, starting transfers between devices, passed_along(): return lax.ppermute(value, axis, pairs)  16.6 us
    dot_general x8, matrix products, one_step(): lax.dot_general(weight_matrices, block_img, (((0,), (0,)), ((), ())), pre...  12.9 us
  transfers between devices with their start and end apart: 19, of which 4 were waited for; matrix products, arithmetic and copies ran while one was open for 27% of the time, Pallas kernels for 0%

commit v1 on v0

v1 whole, which is shorter than its diff:
```python
import jax
import jax.numpy as jnp
from jax import lax
from jax.experimental import pallas as pl
from jax.experimental.pallas import tpu as pltpu
from jax.sharding import PartitionSpec as P

R = 128
H = 64
LOG2E = 1.4426950408889634
NT = (((1,), (1,)), ((), ()))
TN = (((0,), (0,)), ((), ()))
F32 = jnp.float32
BF16 = jnp.bfloat16


def neighbours():
    b, g = lax.axis_index("blk"), lax.axis_index("group")
    z, yl = b // 2, b % 2
    x, rest = g // 4, g % 4
    yh, core = rest // 2, rest % 2
    return {
        "core": (b, x * 4 + yh * 2 + (1 - core)),
        "yh": (b, x * 4 + (1 - yh) * 2 + core),
        "x+": (b, ((x + 1) % 4) * 4 + rest),
        "x-": (b, ((x + 3) % 4) * 4 + rest),
        "yl": (z * 2 + (1 - yl), g),
        "z+": (((z + 1) % 4) * 2 + yl, g),
        "z-": (((z + 3) % 4) * 2 + yl, g),
    }


def kernel(img_ref, txt_ref, wi_ref, wt_ref, ls_ref, bias_ref,
           gfi_ref, gft_ref, gpi_ref, gpt_ref,
           I, T, accI, accT, SC, RC, SXI, SXT, RXI, RXT, RFI, RFT, SY, RY,
           unitI, unitT, invI, invT, ssem, rsem):
    D = img_ref.shape[1]
    near = neighbours()
    barrier = pltpu.get_barrier_semaphore()
    for there in near.values():
        pl.semaphore_signal(barrier, inc=1, device_id=there, device_id_type=pl.DeviceIdType.MESH)

    sent = []

    def send(src, dst, to):
        k = len(sent)
        copy = pltpu.make_async_remote_copy(
            src_ref=src, dst_ref=dst, send_sem=ssem.at[k], recv_sem=rsem.at[k],
            device_id=near[to], device_id_type=pl.DeviceIdType.MESH)
        copy.start()
        sent.append(copy)
        return copy

    def project(feat, w, unit, inv, emb):
        p = jnp.dot(feat[...], w[...], preferred_element_type=F32)
        r = lax.rsqrt(jnp.sum(p * p, axis=1, keepdims=True) + 1e-06)
        u = p * r
        unit[...] = u
        inv[...] = jnp.broadcast_to(r, (R, 128))
        emb[0:R, :] = u.astype(BF16)

    def islot(p, y, c, lo=0, n=R):
        return I.at[pl.ds(((p * 2 + y) * 2 + c) * R + lo, n), :]

    def tslot(p, y, lo=0, n=R):
        return T.at[pl.ds((p * 2 + y) * R + lo, n), :]

    project(img_ref, wi_ref, unitI, invI, I)
    pl.semaphore_wait(barrier, len(near))

    ig, tg, core_in = {}, {}, []

    def spread(got, slot, y, ring):
        got["+", y] = send(slot(0, y), slot(2, y), ring + "+")
        got["-", y] = send(slot(0, y), slot(1, y), ring + "-")

    def halves(got, slot, y, ring):
        got["+", y].wait_recv()
        got["++", y] = send(slot(2, y, 0, H), slot(3, y, 0, H), ring + "+")
        got["-", y].wait_recv()
        got["--", y] = send(slot(1, y, H, H), slot(3, y, H, H), ring + "-")

    own = lambda p, y, lo=0, n=R: islot(p, y, 0, lo, n)

    def to_core(p, y):
        core_in.append(send(islot(p, y, 0), islot(p, y, 1), "core"))

    spread(ig, own, 0, "x")
    ig["y"] = send(own(0, 0), own(0, 1), "yh")
    to_core(0, 0)
    project(txt_ref, wt_ref, unitT, invT, T)
    spread(tg, tslot, 0, "z")
    tg["y"] = send(tslot(0, 0), tslot(0, 1), "yl")
    tg["y"].wait_recv()
    spread(tg, tslot, 1, "z")
    ig["y"].wait_recv()
    spread(ig, own, 1, "x")
    to_core(0, 1)

    scale = jnp.exp(jnp.full((1, 256), ls_ref[0], F32))
    slope = scale * (-LOG2E)
    offset = jnp.full((1, 256), bias_ref[0], F32) * (-LOG2E)

    def unit(p, q, first_i=False, first_t=False, diag=False):
        images = I[pl.ds(pl.multiple_of(p * 512, 512), 512), :]
        texts = T[pl.ds(pl.multiple_of(q * 256, 256), 256), :]
        s = lax.dot_general(images, texts, NT, preferred_element_type=F32)
        e = jnp.exp2(jnp.minimum(s * slope + offset, 126.0))
        if diag:
            row = lax.broadcasted_iota(jnp.int32, e.shape, 0)
            col = lax.broadcasted_iota(jnp.int32, e.shape, 1)
            match = (row == col) & (row < R)
            up = jnp.exp2(jnp.minimum(-(s * slope + offset), 126.0))
            c = jnp.where(match, -1.0 / (1.0 + up), 1.0 / (1.0 + e)).astype(BF16)
        else:
            c = pl.reciprocal(1.0 + e, approx=True).astype(BF16)
        di = jnp.dot(c, texts, preferred_element_type=F32)
        dt = lax.dot_general(c, images, TN, preferred_element_type=F32)
        irows = pl.ds(pl.multiple_of(p * 512, 512), 512)
        trows = pl.ds(pl.multiple_of(q * 256, 256), 256)
        if first_i:
            accI[irows, :] = di
        else:
            accI[irows, :] += di
        if first_t:
            accT[trows, :] = dt
        else:
            accT[trows, :] += dt

    def clear(p, q):
        accI[pl.ds(p * 512, 512), :] = jnp.zeros((512, D), F32)
        accT[pl.ds(q * 256, 256), :] = jnp.zeros((256, D), F32)

    for k in range(1, 4):
        clear(k, k)
    for c in core_in[:2]:
        c.wait_recv()
    halves(tg, tslot, 0, "z")
    halves(ig, own, 0, "x")
    to_core(2, 0)
    to_core(1, 0)
    unit(0, 0, True, True, True)
    halves(tg, tslot, 1, "z")
    halves(ig, own, 1, "x")
    to_core(2, 1)
    to_core(1, 1)
    for c in core_in[2:6]:
        c.wait_recv()

    def middle(k, carry):
        unit(k // 3, k % 3)
        return carry

    lax.fori_loop(1, 9, middle, 0)

    for y in range(2):
        for d in ("++", "--"):
            ig[d, y].wait_recv()
        to_core(3, y)
    for y in range(2):
        for d in ("++", "--"):
            tg[d, y].wait_recv()
    for c in core_in[6:8]:
        c.wait_recv()

    def last_images(k, carry):
        unit(3, k)
        return carry

    lax.fori_loop(0, 4, last_images, 0)

    def rows(n, step):
        def one(k, carry):
            step(k * 16)
            return carry
        lax.fori_loop(0, n // 16, one, 0)

    def at(base, r, n=16):
        return pl.ds(pl.multiple_of(base + r, 16), n)

    core_out = {}

    def core_send(p):
        for y in range(2):
            src, dst = ((p * 2 + y) * 2 + 1) * R, (p * 2 + y) * R

            def step(r, src=src, dst=dst):
                SC[at(dst, r), :] = accI[at(src, r), :].astype(BF16)
            rows(R, step)
            core_out[p, y] = send(SC.at[pl.ds(dst, R), :], RC.at[pl.ds(dst, R), :], "core")

    def core_wait(p):
        for y in range(2):
            core_out[p, y].wait_recv()

    def value_i(p, y, r):
        return accI[at((p * 2 + y) * 2 * R, r), :] + RC[at((p * 2 + y) * R, r), :].astype(F32)

    def value_t(p, y, r):
        return accT[at((p * 2 + y) * R, r), :]

    class Ring:
        def __init__(self, value, stage, rx, rf, axis, n):
            self.value, self.stage, self.rx, self.rf = value, stage, rx, rf
            self.axis, self.n, self.got = axis, n, {}

        def piece(self, p, y, lo, direction, dst, add=None):
            base = (p * 2 + y) * R

            def step(r):
                v = self.value(p, y, lo + r)
                if add is not None:
                    v = v + self.rx[at(add, r), :].astype(F32)
                self.stage[at(base + lo, r), :] = v.astype(BF16)
            rows(H, step)
            return send(self.stage.at[pl.ds(base + lo, H), :], dst, self.axis + direction)

        def far(self):
            for y in range(2):
                self.got["far+", y] = self.piece(3, y, 0, "+", self.rx.at[pl.ds(y * H, H), :])
                self.got["far-", y] = self.piece(3, y, H, "-", self.rx.at[pl.ds((2 + y) * H, H), :])

        def near_plus(self):
            for y in range(2):
                self.got["b+", y] = self.piece(1, y, H, "+", self.rf.at[pl.ds(y * R + H, H), :])

        def near_minus(self):
            for y in range(2):
                self.got["a-", y] = self.piece(2, y, 0, "-", self.rf.at[pl.ds((2 + y) * R, H), :])

        def onward(self):
            for y in range(2):
                self.got["far+", y].wait_recv()
                self.got["a+", y] = self.piece(1, y, 0, "+", self.rf.at[pl.ds(y * R, H), :], y * H)
                self.got["far-", y].wait_recv()
                self.got["b-", y] = self.piece(
                    2, y, H, "-", self.rf.at[pl.ds((2 + y) * R + H, H), :], (2 + y) * H)

        def total(self, y, r):
            return (self.value(0, y, r) + self.rf[at(y * R, r), :].astype(F32)
                    + self.rf[at((2 + y) * R, r), :].astype(F32))

        def cross(self, to):
            for key in ("a+", "b+", "a-", "b-"):
                self.got[key, 1].wait_recv()

            def step(r):
                SY[at(self.n * R, r), :] = self.total(1, r).astype(BF16)
            rows(R, step)
            self.got["y"] = send(SY.at[pl.ds(self.n * R, R), :], RY.at[pl.ds(self.n * R, R), :], to)
            for key in ("a+", "b+", "a-", "b-"):
                self.got[key, 0].wait_recv()

        def finish(self, unit_ref, inv_ref, w_ref, gp_ref, gf_ref):
            self.got["y"].wait_recv()
            t = jnp.exp(jnp.full((1, D), ls_ref[0], F32))

            def step(r):
                g = (self.total(0, r) + RY[at(self.n * R, r), :].astype(F32)) * t
                u = unit_ref[at(0, r), :]
                inv = inv_ref[at(0, r), :][:, 0:1]
                along = jnp.sum(u * g, axis=1, keepdims=True)
                gp_ref[at(0, r), :] = (inv * (g - u * along)).astype(BF16)
            rows(R, step)
            gf_ref[...] = lax.dot_general(
                gp_ref[...], w_ref[...], NT, preferred_element_type=F32).astype(BF16)

    ring_i = Ring(value_i, SXI, RXI, RFI, "x", 0)
    ring_t = Ring(value_t, SXT, RXT, RFT, "z", 1)

    core_send(3)
    unit(1, 3)
    core_send(1)
    core_wait(3)
    ring_i.far()
    unit(2, 3)
    core_send(2)
    core_wait(1)
    ring_i.near_plus()
    unit(0, 3)
    ring_t.far()
    core_send(0)
    core_wait(2)
    ring_i.near_minus()
    ring_t.near_plus()
    ring_t.near_minus()
    core_wait(0)
    ring_i.onward()
    ring_t.onward()
    ring_i.cross("yh")
    ring_t.cross("yl")
    ring_i.finish(unitI, invI, wi_ref, gpi_ref, gfi_ref)
    ring_t.finish(unitT, invT, wt_ref, gpt_ref, gft_ref)
    for copy in sent:
        copy.wait_send()


def fused(img_feat, txt_feat, w_img, w_txt, ls, bias):
    D = img_feat.shape[1]
    vmem = pl.BlockSpec(memory_space=pltpu.VMEM)
    smem = pl.BlockSpec(memory_space=pltpu.SMEM)
    row = jax.ShapeDtypeStruct((R, D), BF16)
    sizes = [(2048, BF16), (1024, BF16), (2048, F32), (1024, F32), (1024, BF16), (1024, BF16),
             (1024, BF16), (1024, BF16), (256, BF16), (256, BF16), (512, BF16), (512, BF16),
             (256, BF16), (256, BF16), (R, F32), (R, F32)]
    return pl.pallas_call(
        kernel,
        out_shape=(row,) * 4,
        in_specs=[vmem] * 4 + [smem] * 2,
        out_specs=(vmem,) * 4,
        scratch_shapes=[pltpu.VMEM((n, D), t) for n, t in sizes]
        + [pltpu.VMEM((R, 128), F32)] * 2
        + [pltpu.SemaphoreType.DMA((72,))] * 2,
        compiler_params=pltpu.CompilerParams(
            collective_id=0, has_side_effects=True, vmem_limit_bytes=60 * 2**20),
    )(img_feat, txt_feat, w_img, w_txt, ls, bias)


def body(img_feat, txt_feat, w_img, w_txt, logit_scale_log, bias):
    gfi, gft, gpi, gpt = fused(img_feat, txt_feat, w_img, w_txt, logit_scale_log, bias)
    img_term = lax.dot_general(img_feat, gpi, TN, preferred_element_type=F32).astype(BF16)
    txt_term = lax.dot_general(txt_feat, gpt, TN, preferred_element_type=F32).astype(BF16)
    both = lax.psum_scatter(jnp.concatenate([img_term, txt_term], axis=1), ("blk", "group"),
                            scatter_dimension=0, tiled=True).astype(F32)
    width = img_feat.shape[1]
    return gfi, gft, both[:, :width], both[:, width:]


def solution(mesh):
    rows = P(("blk", "group"), None)
    return jax.shard_map(
        body, mesh=mesh, in_specs=(rows, rows, P(), P(), P(), P()),
        out_specs=(rows,) * 4, check_vma=False)
```

time: 515 us -> 282 us (0.55)
  waiting for transfers between devices: 299 us -> 154 us
  matrix products: 137 us -> 3.68 us
  Pallas kernels: 0 us -> 101 us
  other arithmetic: 28.5 us -> 4.27 us
  starting transfers between devices: 16.7 us -> 0.04 us
  local copies, waits for them, and re-layouts: 17.1 us -> 3.23 us
    dot_general x30 -> x2, matrix products: 137 us -> 3.68 us  [the longest x1 1.84 us: body(): lax.dot_general(txt_feat, gpt, TN, preferred_element_type=F32).astype(BF16)]
    pallas_call x0 -> x1, Pallas kernels: none -> 101 us  [fused(): pl.pallas_call(kernel, out_shape=(row,) * 4, in_specs=[vmem] * 4 + [smem]...]
    reduce_scatter x1 -> x0, waiting for transfers between devices: 77.1 us -> none  [body(): lax.psum_scatter(image_grad.astype(jnp.bfloat16), 'group', scatter_dimens...]
    all_gather x1 -> x0, waiting for transfers between devices: 58.5 us -> none  [body(): block_img = lax.all_gather(emb_img, 'group', axis=0, tiled=True)]
    ppermute x16 -> x0, starting transfers between devices: 16.6 us -> none  [passed_along(): return lax.ppermute(value, axis, pairs)]
    convert_element_type x13 -> x1, other arithmetic: 17.1 us -> 1.5 us  [body(): both = lax.psum_scatter(jnp.concatenate([img_term, txt_term], axis=1), ('...]
    while x56 -> x0, local copies, waits for them, and re-layouts: 8.26 us -> none
    unnamed x4 -> x2, waiting for transfers between devices: 161 us -> 154 us
  transfers between devices with their start and end apart: 19 -> 1, of which waited for: 4 -> 1; matrix products, arithmetic and copies ran while one was open for 27% -> 0% of each run, Pallas kernels for 0% -> 0%
where the time goes in v1:
time: 282 us
  waiting for transfers between devices  154 us (55%)
  Pallas kernels  101 us (36%)
  between operations  15.5 us (5%)
  other arithmetic  4.27 us (2%)
  matrix products  3.68 us (1%)
  local copies, waits for them, and re-layouts  3.23 us (1%)
    unnamed x2, waiting for transfers between devices  154 us
    pallas_call x1, Pallas kernels, fused(): pl.pallas_call(kernel, out_shape=(row,) * 4, in_specs=[vmem] * 4 + [smem]...  101 us
  transfers between devices with their start and end apart: 1, of which 1 were waited for; matrix products, arithmetic and copies ran while one was open for 0% of the time, Pallas kernels for 0%

profile of v1, /device:TPU:1, one launch (start us, length us, event | category | flops | bytes accessed | tf_op | source)
XLA Modules:
  0.0 282.1 jit_solution(5362013127396241831)
XLA Ops:
  7.2 0.0 copy-start.1
  7.2 0.0 copy-start
  7.2 0.0 all-reduce.3.cloned.1.call-start
  8.6 101.2 %shard_map.93 = (bf16[128,1152]{1,0:T(8,128)(2,1)}, bf16[128,1152]{1,0:T(8,128)(2,1)}, bf16[128,1152]{1,0:T(8,128)(2,1)}, bf16[128,1152]{1,0:T(8,128)(2,1)}) custom-call(bf16[128,1152]{1,0:T(8,128)(2,1)} %img_ref.1, bf16[128,1152]{1,0:T(8,128)(2,1)} %txt_ref.1, bf16[1152,1152]{1,0:T(8,128)(2,1)} %wi_ref.1, bf16[1152,1152]{1,0:T(8,128)(2,1)} %wt_ref.1, ...), custom_call_target="tpu_custom_call" | custom-call | tf_op jit(solution)/shard_map/pallas_call | solution.py:306
  109.8 0.0 copy-done
  109.8 1.8 fusion.1
  111.6 0.0 copy-done.1
  111.6 1.8 fusion
  113.5 2.8 pad_maximum_fusion
  116.3 0.0 copy-start.3
  116.3 0.0 copy-start.2
  116.3 0.0 all-reduce.3.cloned.1.call-update
  116.3 154.2 %all-reduce.3.cloned.1.call-done = bf16[1152,2304]{0,1:T(8,128)(2,1)} async-done(((bf16[1152,2304]{0,1:T(8,128)(2,1)}), bf16[1152,2304]{0,1:T(8,128)(2,1)}) %all-reduce.3.cloned.1.call-update) | async-done | bytes 5308432
  270.5 1.5 dynamic-slice_convert_fusion
  272.0 0.1 fusion.2
  272.1 0.9 copy.12
  272.9 0.9 copy.13
  273.8 0.0 copy-done.3
  273.8 0.7 copy.21
  274.5 0.0 copy-done.2
  274.5 0.7 copy.22
Async XLA Ops:
  7.2 104.5 %copy-start.1 = (bf16[128,1152]{1,0:T(8,128)(2,1)S(1)}, bf16[128,1152]{1,0:T(8,128)(2,1)}, u32[]{:S(2)}) copy-start(bf16[128,1152]{1,0:T(8,128)(2,1)} %img_ref.1) | copy-start | bytes 884740
  7.2 102.6 %copy-start = (bf16[128,1152]{1,0:T(8,128)(2,1)S(1)}, bf16[128,1152]{1,0:T(8,128)(2,1)}, u32[]{:S(2)}) copy-start(bf16[128,1152]{1,0:T(8,128)(2,1)} %txt_ref.1) | copy-start | bytes 884740
  7.2 263.3 %all-reduce.3.cloned.1.call-start = ((), (), s32[]{:S(2)}) async-start(), calls=%async_computation | async-start | bytes 10616832
  116.3 157.5 %copy-start.3 = (bf16[128,1152]{1,0:T(8,128)(2,1)S(1)}, bf16[128,1152]{1,0:T(8,128)(2,1)}, u32[]{:S(2)}) copy-start(bf16[128,1152]{1,0:T(8,128)(2,1)} %get-tuple-element.26) | copy-start | bytes 884740
  116.3 158.2 %copy-start.2 = (bf16[128,1152]{1,0:T(8,128)(2,1)S(1)}, bf16[128,1152]{1,0:T(8,128)(2,1)}, u32[]{:S(2)}) copy-start(bf16[128,1152]{1,0:T(8,128)(2,1)} %get-tuple-element.27) | copy-start | bytes 884740
Sparse Core Ops, SparseCore 0:
  116.4 154.0 all-reduce.2

commit v2 on v1

v2 whole, which is shorter than its diff:
```python
import jax
import jax.numpy as jnp
from jax import lax
from jax.experimental import pallas as pl
from jax.experimental.pallas import tpu as pltpu
from jax.sharding import PartitionSpec as P

R = 128
H = 64
LOG2E = 1.4426950408889634
NT = (((1,), (1,)), ((), ()))
TN = (((0,), (0,)), ((), ()))
F32 = jnp.float32
BF16 = jnp.bfloat16


AXES = (("z", "x", "y"), ("x", "y", "z"), ("y", "z", "x"))
SLOT = 80


def place():
    b, g = lax.axis_index("blk"), lax.axis_index("group")
    return {"x": g // 4, "y": (g // 2) % 2 * 2 + b % 2, "z": b // 2, "core": g % 2}


def neighbours(me):
    def device(**moved):
        c = {**me, **moved}
        return (c["z"] * 2 + c["y"] % 2, c["x"] * 4 + c["y"] // 2 * 2 + c["core"])

    near = {"core": device(core=1 - me["core"])}
    for axis in "xyz":
        for name, step in (("+", 1), ("-", 3), ("2", 2)):
            near[axis + name] = device(**{axis: (me[axis] + step) % 4})
    greeted = list(near.values())
    near["yl"] = device(y=me["y"] + 1 - 2 * (me["y"] % 2))
    return near, greeted


def ring_place(p, here):
    step = jnp.where(p == 1, 1, jnp.where(p == 2, 3, jnp.where(p == 3, 2, 0)))
    return (here + step) & 3


def row_share(axis, v):
    if axis == "y":
        return (v & 1) * 144 + (v >> 1) * 18
    return v * (288 if axis == "z" else 36)


def over(v, step):
    return sum((v >= step * k).astype(jnp.int32) for k in range(1, 4))


def kernel(img_ref, txt_ref, wi_ref, wt_ref, ls_ref, bias_ref,
           gfi_ref, gft_ref, dw_ref,
           I, T, accI, accT, SC, RC, SXI, SXT, RXI, RXT, RFI, RFT, SY, RY,
           unitI, unitT, gpI, gpT, FL, GL, OUT, invI, invT,
           XP, S1, RX1, RF1, S2, RX2, RF2, Z, DM, DR, ssem, rsem):
    D = img_ref.shape[1]
    me = place()
    near, greeted = neighbours(me)
    first = me["core"] == 0
    barrier = pltpu.get_barrier_semaphore()
    for there in greeted:
        pl.semaphore_signal(barrier, inc=1, device_id=there, device_id_type=pl.DeviceIdType.MESH)

    sent = []

    def send(src, dst, to):
        k = len(sent)
        copy = pltpu.make_async_remote_copy(
            src_ref=src, dst_ref=dst, send_sem=ssem.at[k], recv_sem=rsem.at[k],
            device_id=near[to], device_id_type=pl.DeviceIdType.MESH)
        copy.start()
        sent.append(copy)
        return copy

    def project(feat, w, unit, inv, emb):
        p = jnp.dot(feat[...], w[...], preferred_element_type=F32)
        r = lax.rsqrt(jnp.sum(p * p, axis=1, keepdims=True) + 1e-06)
        u = p * r
        unit[...] = u
        inv[...] = jnp.broadcast_to(r, (R, 128))
        emb[0:R, :] = u.astype(BF16)

    def islot(p, y, c, lo=0, n=R):
        return I.at[pl.ds(((p * 2 + y) * 2 + c) * R + lo, n), :]

    def tslot(p, y, lo=0, n=R):
        return T.at[pl.ds((p * 2 + y) * R + lo, n), :]

    project(img_ref, wi_ref, unitI, invI, I)
    pl.semaphore_wait(barrier, len(greeted))

    ig, tg, core_in = {}, {}, []

    def spread(got, slot, y, ring):
        got["+", y] = send(slot(0, y), slot(2, y), ring + "+")
        got["-", y] = send(slot(0, y), slot(1, y), ring + "-")

    def halves(got, slot, y, ring):
        got["+", y].wait_recv()
        got["++", y] = send(slot(2, y, 0, H), slot(3, y, 0, H), ring + "+")
        got["-", y].wait_recv()
        got["--", y] = send(slot(1, y, H, H), slot(3, y, H, H), ring + "-")

    own = lambda p, y, lo=0, n=R: islot(p, y, 0, lo, n)

    def to_core(p, y):
        core_in.append(send(islot(p, y, 0), islot(p, y, 1), "core"))

    spread(ig, own, 0, "x")
    ig["y"] = send(own(0, 0), own(0, 1), "y2")
    to_core(0, 0)
    project(txt_ref, wt_ref, unitT, invT, T)
    FL[0:R, :] = jnp.where(first, img_ref[...], txt_ref[...])
    OUT[...] = jnp.where(first, txt_ref[...], img_ref[...])
    feat_out = send(OUT, FL.at[pl.ds(R, R), :], "core")
    spread(tg, tslot, 0, "z")
    tg["y"] = send(tslot(0, 0), tslot(0, 1), "yl")
    tg["y"].wait_recv()
    spread(tg, tslot, 1, "z")
    ig["y"].wait_recv()
    spread(ig, own, 1, "x")
    to_core(0, 1)

    scale = jnp.exp(jnp.full((1, 256), ls_ref[0], F32))
    slope = scale * (-LOG2E)
    offset = jnp.full((1, 256), bias_ref[0], F32) * (-LOG2E)

    def unit(p, q, first_i=False, first_t=False, diag=False):
        images = I[pl.ds(pl.multiple_of(p * 512, 512), 512), :]
        texts = T[pl.ds(pl.multiple_of(q * 256, 256), 256), :]
        s = lax.dot_general(images, texts, NT, preferred_element_type=F32)
        e = jnp.exp2(jnp.minimum(s * slope + offset, 126.0))
        if diag:
            row = lax.broadcasted_iota(jnp.int32, e.shape, 0)
            col = lax.broadcasted_iota(jnp.int32, e.shape, 1)
            match = (row == col) & (row < R)
            up = jnp.exp2(jnp.minimum(-(s * slope + offset), 126.0))
            c = jnp.where(match, -1.0 / (1.0 + up), 1.0 / (1.0 + e)).astype(BF16)
        else:
            c = pl.reciprocal(1.0 + e, approx=True).astype(BF16)
        di = jnp.dot(c, texts, preferred_element_type=F32)
        dt = lax.dot_general(c, images, TN, preferred_element_type=F32)
        irows = pl.ds(pl.multiple_of(p * 512, 512), 512)
        trows = pl.ds(pl.multiple_of(q * 256, 256), 256)
        if first_i:
            accI[irows, :] = di
        else:
            accI[irows, :] += di
        if first_t:
            accT[trows, :] = dt
        else:
            accT[trows, :] += dt

    def clear(p, q):
        accI[pl.ds(p * 512, 512), :] = jnp.zeros((512, D), F32)
        accT[pl.ds(q * 256, 256), :] = jnp.zeros((256, D), F32)

    for k in range(1, 4):
        clear(k, k)
    feat_out.wait_recv()

    feats = FL[...]
    for third, (a_axis, b_axis, c_axis) in enumerate(AXES):
        def arrange(a, carry):
            s = lax.broadcasted_iota(jnp.int32, (4 * SLOT, 128), 0)
            b = over(s, SLOT)
            k = s - SLOT * b
            c = over(k, 18)
            r = (row_share(a_axis, ring_place(a, me[a_axis]))
                 + row_share(b_axis, ring_place(b, me[b_axis]))
                 + row_share(c_axis, c) + k - 18 * c)
            r = jnp.where(k < 72, r, -1)
            lane = lax.broadcasted_iota(jnp.int32, (4 * SLOT, 128), 1)
            pick = jnp.concatenate(
                [jnp.where(r == lane + 128 * j, 1.0, 0.0).astype(BF16) for j in range(D // 128)],
                axis=1)
            XP[third, pl.ds(pl.multiple_of(a * 4 * SLOT, 16), 4 * SLOT), :] = lax.dot_general(
                pick, feats, NT, preferred_element_type=F32).astype(BF16)
            return carry
        lax.fori_loop(0, 4, arrange, 0)

    for c in core_in[:2]:
        c.wait_recv()
    halves(tg, tslot, 0, "z")
    halves(ig, own, 0, "x")
    to_core(2, 0)
    to_core(1, 0)
    unit(0, 0, True, True, True)
    halves(tg, tslot, 1, "z")
    halves(ig, own, 1, "x")
    to_core(2, 1)
    to_core(1, 1)
    for c in core_in[2:6]:
        c.wait_recv()

    def middle(k, carry):
        unit(k // 3, k % 3)
        return carry

    lax.fori_loop(1, 9, middle, 0)

    for y in range(2):
        for d in ("++", "--"):
            ig[d, y].wait_recv()
        to_core(3, y)
    for y in range(2):
        for d in ("++", "--"):
            tg[d, y].wait_recv()
    for c in core_in[6:8]:
        c.wait_recv()

    def last_images(k, carry):
        unit(3, k)
        return carry

    lax.fori_loop(0, 4, last_images, 0)

    def rows(n, step):
        def one(k, carry):
            step(k * 16)
            return carry
        lax.fori_loop(0, n // 16, one, 0)

    def at(base, r, n=16):
        return pl.ds(pl.multiple_of(base + r, 16), n)

    core_out = {}

    def core_send(p):
        for y in range(2):
            src, dst = ((p * 2 + y) * 2 + 1) * R, (p * 2 + y) * R

            def step(r, src=src, dst=dst):
                SC[at(dst, r), :] = accI[at(src, r), :].astype(BF16)
            rows(R, step)
            core_out[p, y] = send(SC.at[pl.ds(dst, R), :], RC.at[pl.ds(dst, R), :], "core")

    def core_wait(p):
        for y in range(2):
            core_out[p, y].wait_recv()

    def value_i(p, y, r):
        return accI[at((p * 2 + y) * 2 * R, r), :] + RC[at((p * 2 + y) * R, r), :].astype(F32)

    def value_t(p, y, r):
        return accT[at((p * 2 + y) * R, r), :]

    class Ring:
        def __init__(self, axis, n, lo, value, stage, rx, rf):
            self.axis, self.n, self.lo, self.got = axis, n, lo, {}
            self.value, self.stage, self.rx, self.rf = value, stage, rx, rf

        def piece(self, key, p, low, direction, dst, add=None):
            start, n = (0, self.lo) if low else (self.lo, self.n - self.lo)

            def step(r):
                v = self.value(p, start + r)
                if add is not None:
                    v = v + self.rx(add)[at(0, r), :].astype(F32)
                self.stage(p)[at(start, r), :] = v.astype(BF16)
            rows(n, step)
            some = pl.ds(start, n)
            if p == 3:
                some_there = pl.ds(0, n)
            else:
                some_there = some
            self.got[key] = send(self.stage(p).at[some, :], dst.at[some_there, :], self.axis + direction)

        def far(self):
            self.piece("far+", 3, True, "+", self.rx(0))
            self.piece("far-", 3, False, "-", self.rx(1))

        def near_plus(self):
            self.piece("b+", 1, False, "+", self.rf(0))

        def near_minus(self):
            self.piece("a-", 2, True, "-", self.rf(1))

        def onward(self):
            self.got["far+"].wait_recv()
            self.piece("a+", 1, True, "+", self.rf(0), 0)
            self.got["far-"].wait_recv()
            self.piece("b-", 2, False, "-", self.rf(1), 1)

        def arrive(self):
            for key in ("a+", "b+", "a-", "b-"):
                self.got[key].wait_recv()

        def total(self, r):
            return (self.value(0, r) + self.rf(0)[at(0, r), :].astype(F32)
                    + self.rf(1)[at(0, r), :].astype(F32))

    def block_ring(axis, y, value, stage, rx, rf):
        return Ring(
            axis, R, H, lambda p, r: value(p, y, r),
            lambda p: stage.at[pl.ds((p * 2 + y) * R, R), :],
            lambda d: rx.at[pl.ds((d * 2 + y) * H, H), :],
            lambda d: rf.at[pl.ds((d * 2 + y) * R, R), :])

    ring_i = [block_ring("x", y, value_i, SXI, RXI, RFI) for y in range(2)]
    ring_t = [block_ring("z", y, value_t, SXT, RXT, RFT) for y in range(2)]

    def every(rings, what):
        for ring in rings:
            getattr(ring, what)()

    def cross(rings, n, to):
        rings[1].arrive()

        def step(r):
            SY[at(n * R, r), :] = rings[1].total(r).astype(BF16)
        rows(R, step)
        mine = pl.ds(n * R, R)
        return send(SY.at[mine, :], RY.at[mine, :], to)

    def finish(rings, n, crossed, unit_ref, inv_ref, gp):
        rings[0].arrive()
        crossed.wait_recv()
        t = jnp.exp(jnp.full((1, D), ls_ref[0], F32))

        def step(r):
            g = (rings[0].total(r) + RY[at(n * R, r), :].astype(F32)) * t
            u = unit_ref[at(0, r), :]
            inv = inv_ref[at(0, r), :][:, 0:1]
            along = jnp.sum(u * g, axis=1, keepdims=True)
            gp[at(0, r), :] = (inv * (g - u * along)).astype(BF16)
        rows(R, step)

    def feature_grad(gp, w_ref, gf_ref):
        gf_ref[...] = lax.dot_general(
            gp[...], w_ref[...], NT, preferred_element_type=F32).astype(BF16)

    core_send(3)
    unit(1, 3)
    core_send(1)
    core_wait(3)
    every(ring_i, "far")
    unit(2, 3)
    core_send(2)
    core_wait(1)
    every(ring_i, "near_plus")
    unit(0, 3)
    every(ring_t, "far")
    core_send(0)
    core_wait(2)
    every(ring_i, "near_minus")
    every(ring_t, "near_plus")
    every(ring_t, "near_minus")
    core_wait(0)
    every(ring_i, "onward")
    every(ring_t, "onward")
    cross_i = cross(ring_i, 0, "y2")
    cross_t = cross(ring_t, 1, "yl")
    finish(ring_i, 0, cross_i, unitI, invI, gpI)
    finish(ring_t, 1, cross_t, unitT, invT, gpT)

    GL[0:R, :] = jnp.where(first, gpI[...], gpT[...])
    feat_out.wait_send()
    OUT[...] = jnp.where(first, gpT[...], gpI[...])
    grad_in = send(OUT, GL.at[pl.ds(R, R), :], "core")

    def columns(third):
        return slice(third * 384, third * 384 + 384)

    def products(a):
        for third in range(3):
            accI[a * 4 * SLOT:(a + 1) * 4 * SLOT, columns(third)] = jnp.dot(
                XP[third, a * 4 * SLOT:(a + 1) * 4 * SLOT, :], GL[:, columns(third)],
                preferred_element_type=F32)

    def weight_ring(third, axis, n, lo, stage, rx, rf):
        return Ring(
            axis, n, lo, lambda p, r: accI[at(p * n, r), columns(third)],
            lambda p: stage.at[third, pl.ds(p * n, n), :],
            lambda d: rx.at[third, d], lambda d: rf.at[third, d])

    outer = [weight_ring(k, AXES[k][0], 4 * SLOT, 2 * SLOT, S1, RX1, RF1) for k in range(3)]
    inner = [weight_ring(k, AXES[k][1], SLOT, 48, S2, RX2, RF2) for k in range(3)]
    grad_in.wait_recv()
    products(3)
    every(outer, "far")
    products(1)
    every(outer, "near_plus")
    products(2)
    every(outer, "near_minus")
    every(outer, "onward")
    products(0)
    feature_grad(gpI, wi_ref, gfi_ref)
    feature_grad(gpT, wt_ref, gft_ref)
    for third in range(3):
        outer[third].arrive()

        def step(r):
            accI[at(0, r), columns(third)] = outer[third].total(r)
        rows(4 * SLOT, step)
        inner[third].far()
    every(inner, "near_plus")
    every(inner, "near_minus")
    every(inner, "onward")
    last = []
    for third in range(3):
        inner[third].arrive()

        def step(r):
            Z[third, at(0, r), :] = inner[third].total(r).astype(BF16)
        rows(SLOT, step)
        for k, there in enumerate("+-2"):
            last.append(send(Z.at[third, pl.ds(0, SLOT), :],
                             Z.at[third, pl.ds((k + 1) * SLOT, SLOT), :], AXES[third][2] + there))
    for third in range(3):
        for copy in last[third * 3:third * 3 + 3]:
            copy.wait_recv()
        row = lax.broadcasted_iota(jnp.int32, (32, 4 * SLOT), 0)
        k = lax.broadcasted_iota(jnp.int32, (32, 4 * SLOT), 1)
        k = k - SLOT * over(k, SLOT)
        theirs = (row >= 16).astype(jnp.int32)
        i = row - 16 * theirs
        core = theirs + me["core"] - 2 * theirs * me["core"]
        want = me[AXES[third][2]] * 18 + core * 9 + i
        pick = jnp.where((k == want) & (i < 9), 1.0, 0.0).astype(BF16)
        DM[:, columns(third)] = jnp.dot(pick, Z[third], preferred_element_type=F32)
    swap = send(DM.at[pl.ds(16, 16), :], DR, "core")
    swap.wait_recv()
    dw_ref[0:16, :] = jnp.where(first, DM[0:16, :], DR[...])
    dw_ref[16:32, :] = jnp.where(first, DR[...], DM[0:16, :])
    for copy in sent:
        if copy is not feat_out:
            copy.wait_send()


def fused(img_feat, txt_feat, w_img, w_txt, ls, bias):
    D = img_feat.shape[1]
    vmem = pl.BlockSpec(memory_space=pltpu.VMEM)
    smem = pl.BlockSpec(memory_space=pltpu.SMEM)
    row = jax.ShapeDtypeStruct((R, D), BF16)
    sizes = [(2048, BF16), (1024, BF16), (2048, F32), (1024, F32), (1024, BF16), (1024, BF16),
             (1024, BF16), (1024, BF16), (256, BF16), (256, BF16), (512, BF16), (512, BF16),
             (256, BF16), (256, BF16), (R, F32), (R, F32), (R, BF16), (R, BF16),
             (2 * R, BF16), (2 * R, BF16), (R, BF16)]
    thirds = [(4 * 4 * SLOT,), (2, 2 * SLOT), (2, 4 * SLOT), (4 * SLOT,), (2, 48), (2, SLOT),
              (4 * SLOT,)]
    return pl.pallas_call(
        kernel,
        out_shape=(row, row, jax.ShapeDtypeStruct((32, D), F32)),
        in_specs=[vmem] * 4 + [smem] * 2,
        out_specs=(vmem,) * 3,
        scratch_shapes=[pltpu.VMEM((n, D), t) for n, t in sizes]
        + [pltpu.VMEM((R, 128), F32)] * 2
        + [pltpu.VMEM((3, 16 * SLOT, 2 * R), BF16)]
        + [pltpu.VMEM((3,) + n + (D // 3,), BF16) for n in thirds]
        + [pltpu.VMEM((32, D), F32), pltpu.VMEM((16, D), F32)]
        + [pltpu.SemaphoreType.DMA((120,))] * 2,
        compiler_params=pltpu.CompilerParams(
            collective_id=0, has_side_effects=True, vmem_limit_bytes=62 * 2**20),
    )(img_feat, txt_feat, w_img, w_txt, ls, bias)


def body(img_feat, txt_feat, w_img, w_txt, logit_scale_log, bias):
    gfi, gft, dw = fused(img_feat, txt_feat, w_img, w_txt, logit_scale_log, bias)
    return gfi, gft, dw[0:9], dw[16:25]


def solution(mesh):
    rows = P(("blk", "group"), None)
    return jax.shard_map(
        body, mesh=mesh, in_specs=(rows, rows, P(), P(), P(), P()),
        out_specs=(rows,) * 4, check_vma=False)
```

time: 282 us -> 133 us (0.47)
  waiting for transfers between devices: 154 us -> 0 us
  Pallas kernels: 101 us -> 126 us
  between operations: 15.5 us -> 1.93 us
  other arithmetic: 4.27 us -> 0 us
  matrix products: 3.68 us -> 0 us
    unnamed x2 -> x0, waiting for transfers between devices: 154 us -> none
    pallas_call x1, Pallas kernels: 101 us -> 126 us  [fused(): pl.pallas_call(kernel, out_shape=(row, row, jax.ShapeDtypeStruct((32, D),...]
    dot_general x2 -> x0, matrix products: 3.68 us -> none  [the longest x1 1.84 us: body(): lax.dot_general(txt_feat, gpt, TN, preferred_element_type=F32).astype(BF16)]
  transfers between devices with their start and end apart: 1 -> 0, of which waited for: 1 -> 0; matrix products, arithmetic and copies ran while one was open for 0% -> 0% of each run, Pallas kernels for 0% -> 0%
where the time goes in v2:
time: 133 us
  Pallas kernels  126 us (95%)
  local copies, waits for them, and re-layouts  4.98 us (4%)
  between operations  1.93 us (1%)
    pallas_call x1, Pallas kernels, fused(): pl.pallas_call(kernel, out_shape=(row, row, jax.ShapeDtypeStruct((32, D),...  126 us
    unnamed x2, local copies, waits for them, and re-layouts  3.39 us

profile of v2, /device:TPU:1, one launch (start us, length us, event | category | flops | bytes accessed | tf_op | source)
XLA Modules:
  0.0 133.2 jit_solution(7205098784863821218)
XLA Ops:
  1.9 126.3 %shard_map.93 = (bf16[128,1152]{1,0:T(8,128)(2,1)}, bf16[128,1152]{1,0:T(8,128)(2,1)}, f32[32,1152]{1,0:T(8,128)}) custom-call(bf16[128,1152]{1,0:T(8,128)(2,1)} %img_ref.1, bf16[128,1152]{1,0:T(8,128)(2,1)} %txt_ref.1, bf16[1152,1152]{1,0:T(8,128)(2,1)} %wi_ref.1, bf16[1152,1152]{1,0:T(8,128)(2,1)} %wt_ref.1, f32[1]{0:T(128)S(6)} %copy.12.ls_ref, ...), custom_call_target="tpu_custom_call" | custom-call | tf_op jit(solution)/shard_map/pallas_call | solution.py:446
  128.2 1.6 %fusion = (f32[9,1152]{1,0:T(8,128)}, f32[9,1152]{1,0:T(8,128)}) fusion(f32[32,1152]{1,0:T(8,128)} %get-tuple-element.9), kind=kLoop, calls=%fused_computation | loop fusion | bytes 165888 | tf_op jit(solution)/shard_map/slice | solution.py:464
  129.8 1.7 %copy.14 = bf16[128,1152]{1,0:T(8,128)(2,1)} copy(bf16[128,1152]{1,0:T(8,128)(2,1)} %get-tuple-element.16) | data formatting | bytes 589824
  131.5 1.7 %copy.15 = bf16[128,1152]{1,0:T(8,128)(2,1)} copy(bf16[128,1152]{1,0:T(8,128)(2,1)} %get-tuple-element.17) | data formatting | bytes 589824

commit v3 on v2

--- a/solution.py
+++ b/solution.py
@@ -33,7 +33,8 @@
         for name, step in (("+", 1), ("-", 3), ("2", 2)):
             near[axis + name] = device(**{axis: (me[axis] + step) % 4})
     greeted = list(near.values())
-    near["yl"] = device(y=me["y"] + 1 - 2 * (me["y"] % 2))
+    near["yi"] = device(y=me["y"] + 1 - 2 * (me["y"] % 2))
+    near["yt"] = device(y=3 - me["y"])
     return near, greeted
 
 
@@ -52,12 +53,16 @@
     return sum((v >= step * k).astype(jnp.int32) for k in range(1, 4))
 
 
-def kernel(img_ref, txt_ref, wi_ref, wt_ref, ls_ref, bias_ref,
+def kernel(img_hbm, txt_hbm, wi_hbm, wt_hbm, ls_ref, bias_ref,
            gfi_ref, gft_ref, dw_ref,
-           I, T, accI, accT, SC, RC, SXI, SXT, RXI, RXT, RFI, RFT, SY, RY,
+           I, T, accI, accT, SC, RC, SXI, SXT, RXI, RXT, RFI, RFT, SY, RY, SF, RYF, WI, WT, IMG, TXT,
            unitI, unitT, gpI, gpT, FL, GL, OUT, invI, invT,
-           XP, S1, RX1, RF1, S2, RX2, RF2, Z, DM, DR, ssem, rsem):
-    D = img_ref.shape[1]
+           XP, S1, RX1, RF1, S2, RX2, RF2, Z, DM, DR, lsem, ssem, rsem):
+    D = IMG.shape[1]
+    loads = [pltpu.make_async_copy(src, dst, lsem.at[k]) for k, (src, dst) in enumerate(
+        ((img_hbm, IMG), (wi_hbm, WI), (txt_hbm, TXT), (wt_hbm, WT)))]
+    for load in loads:
+        load.start()
     me = place()
     near, greeted = neighbours(me)
     first = me["core"] == 0
@@ -84,46 +89,67 @@
         inv[...] = jnp.broadcast_to(r, (R, 128))
         emb[0:R, :] = u.astype(BF16)
 
-    def islot(p, y, c, lo=0, n=R):
-        return I.at[pl.ds(((p * 2 + y) * 2 + c) * R + lo, n), :]
+    ORDER = ((0, 1), (2, 4), (3, 5), (6, 7))
+
+    def islot(p, y, c=0, lo=0, n=R):
+        return I.at[pl.ds((ORDER[p][y] * 2 + c) * R + lo, n), :]
 
     def tslot(p, y, lo=0, n=R):
-        return T.at[pl.ds((p * 2 + y) * R + lo, n), :]
-
-    project(img_ref, wi_ref, unitI, invI, I)
-    pl.semaphore_wait(barrier, len(greeted))
-
-    ig, tg, core_in = {}, {}, []
+        return T.at[pl.ds(ORDER[p][y] * R + lo, n), :]
+
+    def own(p, y, lo=0, n=R):
+        return islot(p, y, 0, lo, n)
+
+    ig, tg, core_in = {}, {}, {}
 
     def spread(got, slot, y, ring):
         got["+", y] = send(slot(0, y), slot(2, y), ring + "+")
         got["-", y] = send(slot(0, y), slot(1, y), ring + "-")
 
-    def halves(got, slot, y, ring):
+    def near_in(got, y):
         got["+", y].wait_recv()
-        got["++", y] = send(slot(2, y, 0, H), slot(3, y, 0, H), ring + "+")
         got["-", y].wait_recv()
-        got["--", y] = send(slot(1, y, H, H), slot(3, y, H, H), ring + "-")
-
-    own = lambda p, y, lo=0, n=R: islot(p, y, 0, lo, n)
-
-    def to_core(p, y):
-        core_in.append(send(islot(p, y, 0), islot(p, y, 1), "core"))
-
+
+    def onward_halves(got, slot, ring):
+        got["far+"] = send(slot(2, 0, 0, H), slot(3, 0, 0, H), ring + "+")
+        got["far-"] = send(slot(1, 0, H, H), slot(3, 0, H, H), ring + "-")
+
+    def far_in(got, slot, to):
+        got["far+"].wait_recv()
+        got["far-"].wait_recv()
+        got["far y"] = send(slot(3, 0), slot(3, 1), to)
+
+    def to_core(*places):
+        for p, y in places:
+            core_in[p, y] = send(islot(p, y, 0), islot(p, y, 1), "core")
+
+    def from_core(*places):
+        for place_y in places:
+            core_in[place_y].wait_recv()
+
+    loads[0].wait()
+    loads[1].wait()
+    project(IMG, WI, unitI, invI, I)
+    pl.semaphore_wait(barrier, len(greeted))
+    ig["y"] = send(own(0, 0), own(0, 1), "yi")
     spread(ig, own, 0, "x")
-    ig["y"] = send(own(0, 0), own(0, 1), "y2")
-    to_core(0, 0)
-    project(txt_ref, wt_ref, unitT, invT, T)
-    FL[0:R, :] = jnp.where(first, img_ref[...], txt_ref[...])
-    OUT[...] = jnp.where(first, txt_ref[...], img_ref[...])
+    to_core((0, 0))
+    loads[2].wait()
+    loads[3].wait()
+    project(TXT, WT, unitT, invT, T)
+    tg["y"] = send(tslot(0, 0), tslot(0, 1), "yt")
+    spread(tg, tslot, 0, "z")
+    FL[0:R, :] = jnp.where(first, IMG[...], TXT[...])
+    OUT[...] = jnp.where(first, TXT[...], IMG[...])
     feat_out = send(OUT, FL.at[pl.ds(R, R), :], "core")
-    spread(tg, tslot, 0, "z")
-    tg["y"] = send(tslot(0, 0), tslot(0, 1), "yl")
+    accI[512:2048, :] = jnp.zeros((1536, D), F32)
+    accT[256:1024, :] = jnp.zeros((768, D), F32)
+
+    ig["y"].wait_recv()
+    spread(ig, own, 1, "x")
+    to_core((0, 1))
     tg["y"].wait_recv()
     spread(tg, tslot, 1, "z")
-    ig["y"].wait_recv()
-    spread(ig, own, 1, "x")
-    to_core(0, 1)
 
     scale = jnp.exp(jnp.full((1, 256), ls_ref[0], F32))
     slope = scale * (-LOG2E)
@@ -155,14 +181,7 @@
         else:
             accT[trows, :] += dt
 
-    def clear(p, q):
-        accI[pl.ds(p * 512, 512), :] = jnp.zeros((512, D), F32)
-        accT[pl.ds(q * 256, 256), :] = jnp.zeros((256, D), F32)
-
-    for k in range(1, 4):
-        clear(k, k)
     feat_out.wait_recv()
-
     feats = FL[...]
     for third, (a_axis, b_axis, c_axis) in enumerate(AXES):
         def arrange(a, carry):
@@ -183,41 +202,46 @@
             return carry
         lax.fori_loop(0, 4, arrange, 0)
 
-    for c in core_in[:2]:
-        c.wait_recv()
-    halves(tg, tslot, 0, "z")
-    halves(ig, own, 0, "x")
-    to_core(2, 0)
-    to_core(1, 0)
+    near_in(ig, 0)
+    onward_halves(ig, own, "x")
+    to_core((1, 0), (2, 0))
+    near_in(tg, 0)
+    onward_halves(tg, tslot, "z")
+    from_core((0, 0), (0, 1))
     unit(0, 0, True, True, True)
-    halves(tg, tslot, 1, "z")
-    halves(ig, own, 1, "x")
-    to_core(2, 1)
-    to_core(1, 1)
-    for c in core_in[2:6]:
-        c.wait_recv()
-
-    def middle(k, carry):
-        unit(k // 3, k % 3)
+    from_core((1, 0), (2, 0))
+
+    def level1(k, carry):
+        unit(k // 2, k % 2)
         return carry
-
-    lax.fori_loop(1, 9, middle, 0)
-
-    for y in range(2):
-        for d in ("++", "--"):
-            ig[d, y].wait_recv()
-        to_core(3, y)
-    for y in range(2):
-        for d in ("++", "--"):
-            tg[d, y].wait_recv()
-    for c in core_in[6:8]:
-        c.wait_recv()
-
-    def last_images(k, carry):
+    lax.fori_loop(1, 4, level1, 0)
+
+    near_in(ig, 1)
+    to_core((1, 1), (2, 1))
+    near_in(tg, 1)
+    far_in(ig, own, "yi")
+    to_core((3, 0))
+    far_in(tg, tslot, "yt")
+
+    def level2_texts(k, carry):
+        unit(k, 2)
+        return carry
+    lax.fori_loop(0, 2, level2_texts, 0)
+    ig["far y"].wait_recv()
+    to_core((3, 1))
+    from_core((1, 1), (2, 1))
+
+    def level2_images(k, carry):
+        unit(2, k)
+        return carry
+    lax.fori_loop(0, 3, level2_images, 0)
+    tg["far y"].wait_recv()
+    from_core((3, 0), (3, 1))
+
+    def level3_images(k, carry):
         unit(3, k)
         return carry
-
-    lax.fori_loop(0, 4, last_images, 0)
+    lax.fori_loop(0, 4, level3_images, 0)
 
     def rows(n, step):
         def one(k, carry):
@@ -230,65 +254,65 @@
 
     core_out = {}
 
-    def core_send(p):
-        for y in range(2):
-            src, dst = ((p * 2 + y) * 2 + 1) * R, (p * 2 + y) * R
-
-            def step(r, src=src, dst=dst):
-                SC[at(dst, r), :] = accI[at(src, r), :].astype(BF16)
+    def core_send(level):
+        for k in (2 * level, 2 * level + 1):
+            def step(r):
+                SC[at(k * R, r), :] = accI[at((k * 2 + 1) * R, r), :].astype(BF16)
             rows(R, step)
-            core_out[p, y] = send(SC.at[pl.ds(dst, R), :], RC.at[pl.ds(dst, R), :], "core")
-
-    def core_wait(p):
-        for y in range(2):
-            core_out[p, y].wait_recv()
+            block = pl.ds(k * R, R)
+            core_out[k] = send(SC.at[block, :], RC.at[block, :], "core")
+
+    def core_wait(level):
+        core_out[2 * level].wait_recv()
+        core_out[2 * level + 1].wait_recv()
 
     def value_i(p, y, r):
-        return accI[at((p * 2 + y) * 2 * R, r), :] + RC[at((p * 2 + y) * R, r), :].astype(F32)
+        k = ORDER[p][y]
+        return accI[at(k * 2 * R, r), :] + RC[at(k * R, r), :].astype(F32)
 
     def value_t(p, y, r):
-        return accT[at((p * 2 + y) * R, r), :]
+        return accT[at(ORDER[p][y] * R, r), :]
 
     class Ring:
         def __init__(self, axis, n, lo, value, stage, rx, rf):
             self.axis, self.n, self.lo, self.got = axis, n, lo, {}
             self.value, self.stage, self.rx, self.rf = value, stage, rx, rf
 
-        def piece(self, key, p, low, direction, dst, add=None):
-            start, n = (0, self.lo) if low else (self.lo, self.n - self.lo)
-
+        def piece(self, key, p, start, n, direction, dst, dst_start, add=None):
             def step(r):
                 v = self.value(p, start + r)
                 if add is not None:
-                    v = v + self.rx(add)[at(0, r), :].astype(F32)
+                    v = v + add(r).astype(F32)
                 self.stage(p)[at(start, r), :] = v.astype(BF16)
             rows(n, step)
-            some = pl.ds(start, n)
-            if p == 3:
-                some_there = pl.ds(0, n)
-            else:
-                some_there = some
-            self.got[key] = send(self.stage(p).at[some, :], dst.at[some_there, :], self.axis + direction)
-
-        def far(self):
-            self.piece("far+", 3, True, "+", self.rx(0))
-            self.piece("far-", 3, False, "-", self.rx(1))
-
-        def near_plus(self):
-            self.piece("b+", 1, False, "+", self.rf(0))
-
-        def near_minus(self):
-            self.piece("a-", 2, True, "-", self.rf(1))
+            self.got[key] = send(self.stage(p).at[pl.ds(start, n), :],
+                                 dst.at[pl.ds(dst_start, n), :], self.axis + direction)
+
+        def far(self, add=None):
+            lo, hi = self.lo, self.n - self.lo
+            high = None if add is None else lambda r: add(lo + r)
+            self.piece("far+", 3, 0, lo, "+", self.rx(0), 0, add)
+            self.piece("far-", 3, lo, hi, "-", self.rx(1), 0, high)
+
+        def near(self):
+            self.piece("b+", 1, self.lo, self.n - self.lo, "+", self.rf(0), self.lo)
+            self.piece("a-", 2, 0, self.lo, "-", self.rf(1), 0)
+
+        def whole(self):
+            self.piece("a+", 1, 0, self.n, "+", self.rf(0), 0)
+            self.piece("a-", 2, 0, self.n, "-", self.rf(1), 0)
 
         def onward(self):
+            lo, hi = self.lo, self.n - self.lo
             self.got["far+"].wait_recv()
-            self.piece("a+", 1, True, "+", self.rf(0), 0)
+            self.piece("a+", 1, 0, lo, "+", self.rf(0), 0, lambda r: self.rx(0)[at(0, r), :])
             self.got["far-"].wait_recv()
-            self.piece("b-", 2, False, "-", self.rf(1), 1)
+            self.piece("b-", 2, lo, hi, "-", self.rf(1), lo, lambda r: self.rx(1)[at(0, r), :])
 
         def arrive(self):
             for key in ("a+", "b+", "a-", "b-"):
-                self.got[key].wait_recv()
+                if key in self.got:
+                    self.got[key].wait_recv()
 
         def total(self, r):
             return (self.value(0, r) + self.rf(0)[at(0, r), :].astype(F32)
@@ -297,8 +321,8 @@
     def block_ring(axis, y, value, stage, rx, rf):
         return Ring(
             axis, R, H, lambda p, r: value(p, y, r),
-            lambda p: stage.at[pl.ds((p * 2 + y) * R, R), :],
-            lambda d: rx.at[pl.ds((d * 2 + y) * H, H), :],
+            lambda p: stage.at[pl.ds(ORDER[p][y] * R, R), :],
+            lambda d: rx.at[pl.ds(d * H, H), :],
             lambda d: rf.at[pl.ds((d * 2 + y) * R, R), :])
 
     ring_i = [block_ring("x", y, value_i, SXI, RXI, RFI) for y in range(2)]
@@ -334,27 +358,40 @@
         gf_ref[...] = lax.dot_general(
             gp[...], w_ref[...], NT, preferred_element_type=F32).astype(BF16)
 
+    def far_over(ring, n, to):
+        def step(r):
+            SF[at(n * R, r), :] = ring.value(3, r).astype(BF16)
+        rows(R, step)
+        mine = pl.ds(n * R, R)
+        return send(SF.at[mine, :], RYF.at[mine, :], to)
+
+    def far_sum(ring, n, over_y):
+        over_y.wait_recv()
+        ring.far(lambda r: RYF[at(n * R, r), :])
+
     core_send(3)
+    unit(2, 3)
+    core_send(2)
+    core_wait(3)
+    over_i = far_over(ring_i[1], 0, "yi")
     unit(1, 3)
     core_send(1)
-    core_wait(3)
-    every(ring_i, "far")
-    unit(2, 3)
-    core_send(2)
+    core_wait(2)
+    ring_i[1].whole()
+    unit(0, 3)
+    over_t = far_over(ring_t[1], 1, "yt")
+    core_send(0)
+    ring_t[1].whole()
+    far_sum(ring_i[0], 0, over_i)
     core_wait(1)
-    every(ring_i, "near_plus")
-    unit(0, 3)
-    every(ring_t, "far")
-    core_send(0)
-    core_wait(2)
-    every(ring_i, "near_minus")
-    every(ring_t, "near_plus")
-    every(ring_t, "near_minus")
+    ring_i[0].near()
+    ring_t[0].near()
+    far_sum(ring_t[0], 1, over_t)
     core_wait(0)
-    every(ring_i, "onward")
-    every(ring_t, "onward")
-    cross_i = cross(ring_i, 0, "y2")
-    cross_t = cross(ring_t, 1, "yl")
+    cross_i = cross(ring_i, 0, "yi")
+    ring_i[0].onward()
+    cross_t = cross(ring_t, 1, "yt")
+    ring_t[0].onward()
     finish(ring_i, 0, cross_i, unitI, invI, gpI)
     finish(ring_t, 1, cross_t, unitT, invT, gpT)
 
@@ -384,13 +421,12 @@
     products(3)
     every(outer, "far")
     products(1)
-    every(outer, "near_plus")
     products(2)
-    every(outer, "near_minus")
+    every(outer, "near")
     every(outer, "onward")
     products(0)
-    feature_grad(gpI, wi_ref, gfi_ref)
-    feature_grad(gpT, wt_ref, gft_ref)
+    feature_grad(gpI, WI, gfi_ref)
+    feature_grad(gpT, WT, gft_ref)
     for third in range(3):
         outer[third].arrive()
 
@@ -398,8 +434,7 @@
             accI[at(0, r), columns(third)] = outer[third].total(r)
         rows(4 * SLOT, step)
         inner[third].far()
-    every(inner, "near_plus")
-    every(inner, "near_minus")
+    every(inner, "near")
     every(inner, "onward")
     last = []
     for third in range(3):
@@ -435,25 +470,27 @@
 def fused(img_feat, txt_feat, w_img, w_txt, ls, bias):
     D = img_feat.shape[1]
     vmem = pl.BlockSpec(memory_space=pltpu.VMEM)
+    hbm = pl.BlockSpec(memory_space=pl.ANY)
     smem = pl.BlockSpec(memory_space=pltpu.SMEM)
     row = jax.ShapeDtypeStruct((R, D), BF16)
     sizes = [(2048, BF16), (1024, BF16), (2048, F32), (1024, F32), (1024, BF16), (1024, BF16),
-             (1024, BF16), (1024, BF16), (256, BF16), (256, BF16), (512, BF16), (512, BF16),
-             (256, BF16), (256, BF16), (R, F32), (R, F32), (R, BF16), (R, BF16),
+             (1024, BF16), (1024, BF16), (R, BF16), (R, BF16), (512, BF16), (512, BF16),
+             (256, BF16), (256, BF16), (256, BF16), (256, BF16), (D, BF16), (D, BF16),
+             (R, BF16), (R, BF16), (R, F32), (R, F32), (R, BF16), (R, BF16),
              (2 * R, BF16), (2 * R, BF16), (R, BF16)]
     thirds = [(4 * 4 * SLOT,), (2, 2 * SLOT), (2, 4 * SLOT), (4 * SLOT,), (2, 48), (2, SLOT),
               (4 * SLOT,)]
     return pl.pallas_call(
         kernel,
         out_shape=(row, row, jax.ShapeDtypeStruct((32, D), F32)),
-        in_specs=[vmem] * 4 + [smem] * 2,
+        in_specs=[hbm] * 4 + [smem] * 2,
         out_specs=(vmem,) * 3,
         scratch_shapes=[pltpu.VMEM((n, D), t) for n, t in sizes]
         + [pltpu.VMEM((R, 128), F32)] * 2
         + [pltpu.VMEM((3, 16 * SLOT, 2 * R), BF16)]
         + [pltpu.VMEM((3,) + n + (D // 3,), BF16) for n in thirds]
         + [pltpu.VMEM((32, D), F32), pltpu.VMEM((16, D), F32)]
-        + [pltpu.SemaphoreType.DMA((120,))] * 2,
+        + [pltpu.SemaphoreType.DMA((4,))] + [pltpu.SemaphoreType.DMA((120,))] * 2,
         compiler_params=pltpu.CompilerParams(
             collective_id=0, has_side_effects=True, vmem_limit_bytes=62 * 2**20),
     )(img_feat, txt_feat, w_img, w_txt, ls, bias)

time: 133 us -> 115 us (0.86)
  Pallas kernels: 126 us -> 108 us
    pallas_call x1, Pallas kernels: 126 us -> 108 us  [fused(): pl.pallas_call(kernel, out_shape=(row, row, jax.ShapeDtypeStruct((32, D),...]
where the time goes in v3:
time: 115 us
  Pallas kernels  108 us (94%)
  local copies, waits for them, and re-layouts  4.98 us (4%)
  between operations  1.93 us (2%)
    pallas_call x1, Pallas kernels, fused(): pl.pallas_call(kernel, out_shape=(row, row, jax.ShapeDtypeStruct((32, D),...  108 us
    unnamed x2, local copies, waits for them, and re-layouts  3.39 us

profile of v3, /device:TPU:1, one launch (start us, length us, event | category | flops | bytes accessed | tf_op | source)
XLA Modules:
  0.0 114.8 jit_solution(11776454635352197928)
XLA Ops:
  1.9 107.8 %shard_map.93 = (bf16[128,1152]{1,0:T(8,128)(2,1)}, bf16[128,1152]{1,0:T(8,128)(2,1)}, f32[32,1152]{1,0:T(8,128)}) custom-call(bf16[128,1152]{1,0:T(8,128)(2,1)} %img_hbm.1, bf16[128,1152]{1,0:T(8,128)(2,1)} %txt_hbm.1, bf16[1152,1152]{1,0:T(8,128)(2,1)} %wi_hbm.1, bf16[1152,1152]{1,0:T(8,128)(2,1)} %wt_hbm.1, f32[1]{0:T(128)S(6)} %copy.12.ls_ref, ...), custom_call_target="tpu_custom_call" | custom-call | tf_op jit(solution)/shard_map/pallas_call | solution.py:483
  109.8 1.6 %fusion = (f32[9,1152]{1,0:T(8,128)}, f32[9,1152]{1,0:T(8,128)}) fusion(f32[32,1152]{1,0:T(8,128)} %get-tuple-element.9), kind=kLoop, calls=%fused_computation | loop fusion | bytes 165888 | tf_op jit(solution)/shard_map/slice | solution.py:501
  111.4 1.7 %copy.14 = bf16[128,1152]{1,0:T(8,128)(2,1)} copy(bf16[128,1152]{1,0:T(8,128)(2,1)} %get-tuple-element.16) | data formatting | bytes 589824
  113.1 1.7 %copy.15 = bf16[128,1152]{1,0:T(8,128)(2,1)} copy(bf16[128,1152]{1,0:T(8,128)(2,1)} %get-tuple-element.17) | data formatting | bytes 589824

commit v4 on v3

--- a/solution.py
+++ b/solution.py
@@ -54,10 +54,10 @@
 
 
 def kernel(img_hbm, txt_hbm, wi_hbm, wt_hbm, ls_ref, bias_ref,
-           gfi_ref, gft_ref, dw_ref,
+           gf_ref, dw_ref,
            I, T, accI, accT, SC, RC, SXI, SXT, RXI, RXT, RFI, RFT, SY, RY, SF, RYF, WI, WT, IMG, TXT,
            unitI, unitT, gpI, gpT, FL, GL, OUT, invI, invT,
-           XP, S1, RX1, RF1, S2, RX2, RF2, Z, DM, DR, lsem, ssem, rsem):
+           XP, S1, RX1, RF1, S2, RF2, Z, DM, DR, lsem, ssem, rsem):
     D = IMG.shape[1]
     loads = [pltpu.make_async_copy(src, dst, lsem.at[k]) for k, (src, dst) in enumerate(
         ((img_hbm, IMG), (wi_hbm, WI), (txt_hbm, TXT), (wt_hbm, WT)))]
@@ -142,44 +142,44 @@
     FL[0:R, :] = jnp.where(first, IMG[...], TXT[...])
     OUT[...] = jnp.where(first, TXT[...], IMG[...])
     feat_out = send(OUT, FL.at[pl.ds(R, R), :], "core")
-    accI[512:2048, :] = jnp.zeros((1536, D), F32)
-    accT[256:1024, :] = jnp.zeros((768, D), F32)
-
+    accT[768:1024, :] = jnp.zeros((256, D), F32)
+
+    near_in(ig, 0)
+    onward_halves(ig, own, "x")
+    to_core((1, 0), (2, 0))
+    near_in(tg, 0)
+    onward_halves(tg, tslot, "z")
     ig["y"].wait_recv()
     spread(ig, own, 1, "x")
     to_core((0, 1))
     tg["y"].wait_recv()
     spread(tg, tslot, 1, "z")
 
-    scale = jnp.exp(jnp.full((1, 256), ls_ref[0], F32))
+    scale = jnp.exp(jnp.full((1, 512), ls_ref[0], F32))
     slope = scale * (-LOG2E)
-    offset = jnp.full((1, 256), bias_ref[0], F32) * (-LOG2E)
-
-    def unit(p, q, first_i=False, first_t=False, diag=False):
-        images = I[pl.ds(pl.multiple_of(p * 512, 512), 512), :]
-        texts = T[pl.ds(pl.multiple_of(q * 256, 256), 256), :]
-        s = lax.dot_general(images, texts, NT, preferred_element_type=F32)
-        e = jnp.exp2(jnp.minimum(s * slope + offset, 126.0))
-        if diag:
-            row = lax.broadcasted_iota(jnp.int32, e.shape, 0)
-            col = lax.broadcasted_iota(jnp.int32, e.shape, 1)
-            match = (row == col) & (row < R)
-            up = jnp.exp2(jnp.minimum(-(s * slope + offset), 126.0))
-            c = jnp.where(match, -1.0 / (1.0 + up), 1.0 / (1.0 + e)).astype(BF16)
-        else:
-            c = pl.reciprocal(1.0 + e, approx=True).astype(BF16)
+    offset = jnp.full((1, 512), bias_ref[0], F32) * (-LOG2E)
+
+    def unit(ilo, m, tlo, n, new_i=False, new_t=False, diag=False):
+        irows, trows = slice(ilo, ilo + m), slice(tlo, tlo + n)
+        images, texts = I[irows, :], T[trows, :]
+        parts = []
+        for k in range(0, m, 256):
+            s = lax.dot_general(I[ilo + k:ilo + k + 256, :], texts, NT, preferred_element_type=F32)
+            x = s * slope[:, :n] + offset[:, :n]
+            c = pltpu.reciprocal(1.0 + jnp.exp2(jnp.minimum(x, 126.0)), approx=True).astype(BF16)
+            if diag and k == 0:
+                up = jnp.exp2(jnp.minimum(-x[:R, :R], 126.0))
+                row = lax.broadcasted_iota(jnp.int32, (R, R), 0)
+                col = lax.broadcasted_iota(jnp.int32, (R, R), 1)
+                corner = jnp.where(row == col, -1.0 / (1.0 + up), c[:R, :R].astype(F32)).astype(BF16)
+                c = jnp.concatenate(
+                    [jnp.concatenate([corner, c[:R, R:]], axis=1), c[R:, :]], axis=0)
+            parts.append(c)
+        c = jnp.concatenate(parts, axis=0)
         di = jnp.dot(c, texts, preferred_element_type=F32)
         dt = lax.dot_general(c, images, TN, preferred_element_type=F32)
-        irows = pl.ds(pl.multiple_of(p * 512, 512), 512)
-        trows = pl.ds(pl.multiple_of(q * 256, 256), 256)
-        if first_i:
-            accI[irows, :] = di
-        else:
-            accI[irows, :] += di
-        if first_t:
-            accT[trows, :] = dt
-        else:
-            accT[trows, :] += dt
+        accI[irows, :] = di if new_i else accI[irows, :] + di
+        accT[trows, :] = dt if new_t else accT[trows, :] + dt
 
     feat_out.wait_recv()
     feats = FL[...]
@@ -202,46 +202,23 @@
             return carry
         lax.fori_loop(0, 4, arrange, 0)
 
-    near_in(ig, 0)
-    onward_halves(ig, own, "x")
-    to_core((1, 0), (2, 0))
-    near_in(tg, 0)
-    onward_halves(tg, tslot, "z")
-    from_core((0, 0), (0, 1))
-    unit(0, 0, True, True, True)
-    from_core((1, 0), (2, 0))
-
-    def level1(k, carry):
-        unit(k // 2, k % 2)
-        return carry
-    lax.fori_loop(1, 4, level1, 0)
-
+    far_in(ig, own, "yi")
+    to_core((3, 0))
+    far_in(tg, tslot, "yt")
+    from_core((0, 0), (0, 1), (1, 0), (2, 0))
+    unit(0, 1024, 0, 512, True, True, True)
     near_in(ig, 1)
     to_core((1, 1), (2, 1))
     near_in(tg, 1)
-    far_in(ig, own, "yi")
-    to_core((3, 0))
-    far_in(tg, tslot, "yt")
-
-    def level2_texts(k, carry):
-        unit(k, 2)
-        return carry
-    lax.fori_loop(0, 2, level2_texts, 0)
+    unit(0, 1024, 512, 256, False, True)
     ig["far y"].wait_recv()
     to_core((3, 1))
     from_core((1, 1), (2, 1))
-
-    def level2_images(k, carry):
-        unit(2, k)
-        return carry
-    lax.fori_loop(0, 3, level2_images, 0)
+    unit(1024, 512, 0, 512, True)
     tg["far y"].wait_recv()
     from_core((3, 0), (3, 1))
-
-    def level3_images(k, carry):
-        unit(3, k)
-        return carry
-    lax.fori_loop(0, 4, level3_images, 0)
+    unit(1536, 512, 0, 512, True)
+    unit(1536, 512, 512, 512)
 
     def rows(n, step):
         def one(k, carry):
@@ -274,7 +251,8 @@
         return accT[at(ORDER[p][y] * R, r), :]
 
     class Ring:
-        def __init__(self, axis, n, lo, value, stage, rx, rf):
+        def __init__(self, axis, n, lo, value, stage, rx, rf, sources=2):
+            self.sources = sources
             self.axis, self.n, self.lo, self.got = axis, n, lo, {}
             self.value, self.stage, self.rx, self.rf = value, stage, rx, rf
 
@@ -302,6 +280,10 @@
             self.piece("a+", 1, 0, self.n, "+", self.rf(0), 0)
             self.piece("a-", 2, 0, self.n, "-", self.rf(1), 0)
 
+        def direct(self):
+            for k, (p, there) in enumerate(((3, "2"), (1, "+"), (2, "-"))):
+                self.piece(there, p, 0, self.n, there, self.rf(k), 0)
+
         def onward(self):
             lo, hi = self.lo, self.n - self.lo
             self.got["far+"].wait_recv()
@@ -310,13 +292,15 @@
             self.piece("b-", 2, lo, hi, "-", self.rf(1), lo, lambda r: self.rx(1)[at(0, r), :])
 
         def arrive(self):
-            for key in ("a+", "b+", "a-", "b-"):
+            for key in ("a+", "b+", "a-", "b-", "+", "-", "2"):
                 if key in self.got:
                     self.got[key].wait_recv()
 
         def total(self, r):
-            return (self.value(0, r) + self.rf(0)[at(0, r), :].astype(F32)
-                    + self.rf(1)[at(0, r), :].astype(F32))
+            v = self.value(0, r)
+            for k in range(self.sources):
+                v = v + self.rf(k)[at(0, r), :].astype(F32)
+            return v
 
     def block_ring(axis, y, value, stage, rx, rf):
         return Ring(
@@ -354,8 +338,8 @@
             gp[at(0, r), :] = (inv * (g - u * along)).astype(BF16)
         rows(R, step)
 
-    def feature_grad(gp, w_ref, gf_ref):
-        gf_ref[...] = lax.dot_general(
+    def feature_grad(gp, w_ref, lo):
+        gf_ref[lo:lo + R, :] = lax.dot_general(
             gp[...], w_ref[...], NT, preferred_element_type=F32).astype(BF16)
 
     def far_over(ring, n, to):
@@ -370,16 +354,15 @@
         ring.far(lambda r: RYF[at(n * R, r), :])
 
     core_send(3)
-    unit(2, 3)
+    unit(1024, 512, 512, 512)
     core_send(2)
     core_wait(3)
     over_i = far_over(ring_i[1], 0, "yi")
-    unit(1, 3)
-    core_send(1)
     core_wait(2)
     ring_i[1].whole()
-    unit(0, 3)
+    unit(0, 1024, 768, 256)
     over_t = far_over(ring_t[1], 1, "yt")
+    core_send(1)
     core_send(0)
     ring_t[1].whole()
     far_sum(ring_i[0], 0, over_i)
@@ -409,14 +392,14 @@
                 XP[third, a * 4 * SLOT:(a + 1) * 4 * SLOT, :], GL[:, columns(third)],
                 preferred_element_type=F32)
 
-    def weight_ring(third, axis, n, lo, stage, rx, rf):
+    def weight_ring(third, axis, n, lo, stage, rx, rf, sources):
         return Ring(
             axis, n, lo, lambda p, r: accI[at(p * n, r), columns(third)],
             lambda p: stage.at[third, pl.ds(p * n, n), :],
-            lambda d: rx.at[third, d], lambda d: rf.at[third, d])
-
-    outer = [weight_ring(k, AXES[k][0], 4 * SLOT, 2 * SLOT, S1, RX1, RF1) for k in range(3)]
-    inner = [weight_ring(k, AXES[k][1], SLOT, 48, S2, RX2, RF2) for k in range(3)]
+            lambda d: rx.at[third, d], lambda d: rf.at[third, d], sources)
+
+    outer = [weight_ring(k, AXES[k][0], 4 * SLOT, 2 * SLOT, S1, RX1, RF1, 2) for k in range(3)]
+    inner = [weight_ring(k, AXES[k][1], SLOT, 0, S2, None, RF2, 3) for k in range(3)]
     grad_in.wait_recv()
     products(3)
     every(outer, "far")
@@ -425,17 +408,15 @@
     every(outer, "near")
     every(outer, "onward")
     products(0)
-    feature_grad(gpI, WI, gfi_ref)
-    feature_grad(gpT, WT, gft_ref)
+    feature_grad(gpI, WI, 0)
+    feature_grad(gpT, WT, R)
     for third in range(3):
         outer[third].arrive()
 
         def step(r):
             accI[at(0, r), columns(third)] = outer[third].total(r)
         rows(4 * SLOT, step)
-        inner[third].far()
-    every(inner, "near")
-    every(inner, "onward")
+        inner[third].direct()
     last = []
     for third in range(3):
         inner[third].arrive()
@@ -472,19 +453,18 @@
     vmem = pl.BlockSpec(memory_space=pltpu.VMEM)
     hbm = pl.BlockSpec(memory_space=pl.ANY)
     smem = pl.BlockSpec(memory_space=pltpu.SMEM)
-    row = jax.ShapeDtypeStruct((R, D), BF16)
     sizes = [(2048, BF16), (1024, BF16), (2048, F32), (1024, F32), (1024, BF16), (1024, BF16),
              (1024, BF16), (1024, BF16), (R, BF16), (R, BF16), (512, BF16), (512, BF16),
              (256, BF16), (256, BF16), (256, BF16), (256, BF16), (D, BF16), (D, BF16),
              (R, BF16), (R, BF16), (R, F32), (R, F32), (R, BF16), (R, BF16),
              (2 * R, BF16), (2 * R, BF16), (R, BF16)]
-    thirds = [(4 * 4 * SLOT,), (2, 2 * SLOT), (2, 4 * SLOT), (4 * SLOT,), (2, 48), (2, SLOT),
+    thirds = [(4 * 4 * SLOT,), (2, 2 * SLOT), (2, 4 * SLOT), (4 * SLOT,), (3, SLOT),
               (4 * SLOT,)]
     return pl.pallas_call(
         kernel,
-        out_shape=(row, row, jax.ShapeDtypeStruct((32, D), F32)),
+        out_shape=(jax.ShapeDtypeStruct((2 * R, D), BF16), jax.ShapeDtypeStruct((32, D), F32)),
         in_specs=[hbm] * 4 + [smem] * 2,
-        out_specs=(vmem,) * 3,
+        out_specs=(vmem,) * 2,
         scratch_shapes=[pltpu.VMEM((n, D), t) for n, t in sizes]
         + [pltpu.VMEM((R, 128), F32)] * 2
         + [pltpu.VMEM((3, 16 * SLOT, 2 * R), BF16)]
@@ -497,8 +477,8 @@
 
 
 def body(img_feat, txt_feat, w_img, w_txt, logit_scale_log, bias):
-    gfi, gft, dw = fused(img_feat, txt_feat, w_img, w_txt, logit_scale_log, bias)
-    return gfi, gft, dw[0:9], dw[16:25]
+    gf, dw = fused(img_feat, txt_feat, w_img, w_txt, logit_scale_log, bias)
+    return gf[:R], gf[R:], dw[0:9], dw[16:25]
 
 
 def solution(mesh):

time: 115 us -> 101 us (0.88)
  Pallas kernels: 108 us -> 95.8 us
  local copies, waits for them, and re-layouts: 4.98 us -> 3.49 us
    pallas_call x1, Pallas kernels: 108 us -> 95.8 us  [fused(): pl.pallas_call(kernel, out_shape=(jax.ShapeDtypeStruct((2 * R, D), BF16),...]
    unnamed x2 -> x0, local copies, waits for them, and re-layouts: 3.39 us -> none
    slice x1 -> x2, local copies, waits for them, and re-layouts: 1.58 us -> 3.49 us  [body(): return (gf[:R], gf[R:], dw[0:9], dw[16:25])]
where the time goes in v4:
time: 101 us
  Pallas kernels  95.8 us (95%)
  local copies, waits for them, and re-layouts  3.49 us (3%)
  between operations  1.93 us (2%)
    pallas_call x1, Pallas kernels, fused(): pl.pallas_call(kernel, out_shape=(jax.ShapeDtypeStruct((2 * R, D), BF16),...  95.8 us
    slice x2, local copies, waits for them, and re-layouts, body(): return (gf[:R], gf[R:], dw[0:9], dw[16:25])  3.49 us

profile of v4, /device:TPU:1, one launch (start us, length us, event | category | flops | bytes accessed | tf_op | source)
XLA Modules:
  0.0 101.2 jit_solution(6601656694336904332)
XLA Ops:
  1.9 95.8 %shard_map.93 = (bf16[256,1152]{1,0:T(8,128)(2,1)}, f32[32,1152]{1,0:T(8,128)}) custom-call(bf16[128,1152]{1,0:T(8,128)(2,1)} %img_hbm.1, bf16[128,1152]{1,0:T(8,128)(2,1)} %txt_hbm.1, bf16[1152,1152]{1,0:T(8,128)(2,1)} %wi_hbm.1, bf16[1152,1152]{1,0:T(8,128)(2,1)} %wt_hbm.1, f32[1]{0:T(128)S(6)} %copy.10.ls_ref, f32[1]{0:T(128)S(6)} %copy.11.bias_ref), custom_call_target="tpu_custom_call" | custom-call | tf_op jit(solution)/shard_map/pallas_call | solution.py:463
  97.7 1.9 %fusion = (bf16[128,1152]{1,0:T(8,128)(2,1)}, bf16[128,1152]{1,0:T(8,128)(2,1)}) fusion(bf16[256,1152]{1,0:T(8,128)(2,1)} %get-tuple-element.6), kind=kLoop, calls=%fused_computation | loop fusion | bytes 1179648 | tf_op jit(solution)/shard_map/slice | solution.py:481
  99.6 1.6 %fusion.1 = (f32[9,1152]{1,0:T(8,128)}, f32[9,1152]{1,0:T(8,128)}) fusion(f32[32,1152]{1,0:T(8,128)} %get-tuple-element.7), kind=kLoop, calls=%fused_computation.1 | loop fusion | bytes 165888 | tf_op jit(solution)/shard_map/slice | solution.py:481

commit v5 on v4

--- a/solution.py
+++ b/solution.py
@@ -31,7 +31,9 @@
     near = {"core": device(core=1 - me["core"])}
     for axis in "xyz":
         for name, step in (("+", 1), ("-", 3), ("2", 2)):
-            near[axis + name] = device(**{axis: (me[axis] + step) % 4})
+            moved = {axis: (me[axis] + step) % 4}
+            near[axis + name] = device(**moved)
+            near[axis + name + "c"] = device(**moved, core=1 - me["core"])
     greeted = list(near.values())
     near["yi"] = device(y=me["y"] + 1 - 2 * (me["y"] % 2))
     near["yt"] = device(y=3 - me["y"])
@@ -57,7 +59,7 @@
            gf_ref, dw_ref,
            I, T, accI, accT, SC, RC, SXI, SXT, RXI, RXT, RFI, RFT, SY, RY, SF, RYF, WI, WT, IMG, TXT,
            unitI, unitT, gpI, gpT, FL, GL, OUT, invI, invT,
-           XP, S1, RX1, RF1, S2, RF2, Z, DM, DR, lsem, ssem, rsem):
+           XP, S1, RX1, RF1, S2, RF2, E, Z, lsem, ssem, rsem):
     D = IMG.shape[1]
     loads = [pltpu.make_async_copy(src, dst, lsem.at[k]) for k, (src, dst) in enumerate(
         ((img_hbm, IMG), (wi_hbm, WI), (txt_hbm, TXT), (wt_hbm, WT)))]
@@ -143,6 +145,27 @@
     OUT[...] = jnp.where(first, TXT[...], IMG[...])
     feat_out = send(OUT, FL.at[pl.ds(R, R), :], "core")
     accT[768:1024, :] = jnp.zeros((256, D), F32)
+
+    feat_out.wait_recv()
+    feats = FL[...]
+    for third, (a_axis, b_axis, c_axis) in enumerate(AXES):
+        def arrange(a, carry):
+            s = lax.broadcasted_iota(jnp.int32, (4 * SLOT, 128), 0)
+            b = over(s, SLOT)
+            k = s - SLOT * b
+            c = over(k, 18)
+            r = (row_share(a_axis, ring_place(a, me[a_axis]))
+                 + row_share(b_axis, ring_place(b, me[b_axis]))
+                 + row_share(c_axis, c) + k - 18 * c)
+            r = jnp.where(k < 72, r, -1)
+            lane = lax.broadcasted_iota(jnp.int32, (4 * SLOT, 128), 1)
+            pick = jnp.concatenate(
+                [jnp.where(r == lane + 128 * j, 1.0, 0.0).astype(BF16) for j in range(D // 128)],
+                axis=1)
+            XP[third, pl.ds(pl.multiple_of(a * 4 * SLOT, 16), 4 * SLOT), :] = lax.dot_general(
+                pick, feats, NT, preferred_element_type=F32).astype(BF16)
+            return carry
+        lax.fori_loop(0, 4, arrange, 0)
 
     near_in(ig, 0)
     onward_halves(ig, own, "x")
@@ -181,27 +204,6 @@
         accI[irows, :] = di if new_i else accI[irows, :] + di
         accT[trows, :] = dt if new_t else accT[trows, :] + dt
 
-    feat_out.wait_recv()
-    feats = FL[...]
-    for third, (a_axis, b_axis, c_axis) in enumerate(AXES):
-        def arrange(a, carry):
-            s = lax.broadcasted_iota(jnp.int32, (4 * SLOT, 128), 0)
-            b = over(s, SLOT)
-            k = s - SLOT * b
-            c = over(k, 18)
-            r = (row_share(a_axis, ring_place(a, me[a_axis]))
-                 + row_share(b_axis, ring_place(b, me[b_axis]))
-                 + row_share(c_axis, c) + k - 18 * c)
-            r = jnp.where(k < 72, r, -1)
-            lane = lax.broadcasted_iota(jnp.int32, (4 * SLOT, 128), 1)
-            pick = jnp.concatenate(
-                [jnp.where(r == lane + 128 * j, 1.0, 0.0).astype(BF16) for j in range(D // 128)],
-                axis=1)
-            XP[third, pl.ds(pl.multiple_of(a * 4 * SLOT, 16), 4 * SLOT), :] = lax.dot_general(
-                pick, feats, NT, preferred_element_type=F32).astype(BF16)
-            return carry
-        lax.fori_loop(0, 4, arrange, 0)
-
     far_in(ig, own, "yi")
     to_core((3, 0))
     far_in(tg, tslot, "yt")
@@ -215,26 +217,27 @@
     to_core((3, 1))
     from_core((1, 1), (2, 1))
     unit(1024, 512, 0, 512, True)
+    unit(1024, 512, 512, 256)
     tg["far y"].wait_recv()
     from_core((3, 0), (3, 1))
     unit(1536, 512, 0, 512, True)
     unit(1536, 512, 512, 512)
 
-    def rows(n, step):
+    def rows(n, step, size=32):
         def one(k, carry):
-            step(k * 16)
+            step(k * size, size)
             return carry
-        lax.fori_loop(0, n // 16, one, 0)
-
-    def at(base, r, n=16):
+        lax.fori_loop(0, n // size, one, 0)
+
+    def at(base, r, n):
         return pl.ds(pl.multiple_of(base + r, 16), n)
 
     core_out = {}
 
     def core_send(level):
         for k in (2 * level, 2 * level + 1):
-            def step(r):
-                SC[at(k * R, r), :] = accI[at((k * 2 + 1) * R, r), :].astype(BF16)
+            def step(r, w):
+                SC[at(k * R, r, w), :] = accI[at((k * 2 + 1) * R, r, w), :].astype(BF16)
             rows(R, step)
             block = pl.ds(k * R, R)
             core_out[k] = send(SC.at[block, :], RC.at[block, :], "core")
@@ -243,32 +246,35 @@
         core_out[2 * level].wait_recv()
         core_out[2 * level + 1].wait_recv()
 
-    def value_i(p, y, r):
+    def value_i(p, y, r, w):
         k = ORDER[p][y]
-        return accI[at(k * 2 * R, r), :] + RC[at(k * R, r), :].astype(F32)
-
-    def value_t(p, y, r):
-        return accT[at(ORDER[p][y] * R, r), :]
+        return accI[at(k * 2 * R, r, w), :] + RC[at(k * R, r, w), :].astype(F32)
+
+    def value_t(p, y, r, w):
+        return accT[at(ORDER[p][y] * R, r, w), :]
 
     class Ring:
-        def __init__(self, axis, n, lo, value, stage, rx, rf, sources=2):
-            self.sources = sources
+        def __init__(self, axis, n, lo, value, stage, rx, rf, sources=2, size=32):
+            self.sources, self.size = sources, size
             self.axis, self.n, self.lo, self.got = axis, n, lo, {}
             self.value, self.stage, self.rx, self.rf = value, stage, rx, rf
 
         def piece(self, key, p, start, n, direction, dst, dst_start, add=None):
-            def step(r):
-                v = self.value(p, start + r)
+            def step(r, w):
+                v = self.value(p, start + r, w)
                 if add is not None:
-                    v = v + add(r).astype(F32)
-                self.stage(p)[at(start, r), :] = v.astype(BF16)
-            rows(n, step)
+                    v = v + add(r, w).astype(F32)
+                self.stage(p)[at(start, r, w), :] = v.astype(BF16)
+            rows(n, step, self.size)
+            self.launch(key, p, start, n, direction, dst, dst_start)
+
+        def launch(self, key, p, start, n, direction, dst, dst_start):
             self.got[key] = send(self.stage(p).at[pl.ds(start, n), :],
                                  dst.at[pl.ds(dst_start, n), :], self.axis + direction)
 
         def far(self, add=None):
             lo, hi = self.lo, self.n - self.lo
-            high = None if add is None else lambda r: add(lo + r)
+            high = None if add is None else lambda r, w: add(lo + r, w)
             self.piece("far+", 3, 0, lo, "+", self.rx(0), 0, add)
             self.piece("far-", 3, lo, hi, "-", self.rx(1), 0, high)
 
@@ -287,24 +293,33 @@
         def onward(self):
             lo, hi = self.lo, self.n - self.lo
             self.got["far+"].wait_recv()
-            self.piece("a+", 1, 0, lo, "+", self.rf(0), 0, lambda r: self.rx(0)[at(0, r), :])
+            self.piece("a+", 1, 0, lo, "+", self.rf(0), 0, lambda r, w: self.rx(0)[at(0, r, w), :])
             self.got["far-"].wait_recv()
-            self.piece("b-", 2, lo, hi, "-", self.rf(1), lo, lambda r: self.rx(1)[at(0, r), :])
+            self.piece("b-", 2, lo, hi, "-", self.rf(1), lo, lambda r, w: self.rx(1)[at(0, r, w), :])
 
         def arrive(self):
             for key in ("a+", "b+", "a-", "b-", "+", "-", "2"):
                 if key in self.got:
                     self.got[key].wait_recv()
 
-        def total(self, r):
-            v = self.value(0, r)
+        def staged_far(self):
+            lo, hi = self.lo, self.n - self.lo
+            self.launch("far+", 3, 0, lo, "+", self.rx(0), 0)
+            self.launch("far-", 3, lo, hi, "-", self.rx(1), 0)
+
+        def staged_near(self):
+            self.launch("b+", 1, self.lo, self.n - self.lo, "+", self.rf(0), self.lo)
+            self.launch("a-", 2, 0, self.lo, "-", self.rf(1), 0)
+
+        def total(self, r, w):
+            v = self.value(0, r, w)
             for k in range(self.sources):
-                v = v + self.rf(k)[at(0, r), :].astype(F32)
+                v = v + self.rf(k)[at(0, r, w), :].astype(F32)
             return v
 
     def block_ring(axis, y, value, stage, rx, rf):
         return Ring(
-            axis, R, H, lambda p, r: value(p, y, r),
+            axis, R, H, lambda p, r, w: value(p, y, r, w),
             lambda p: stage.at[pl.ds(ORDER[p][y] * R, R), :],
             lambda d: rx.at[pl.ds(d * H, H), :],
             lambda d: rf.at[pl.ds((d * 2 + y) * R, R), :])
@@ -319,8 +334,8 @@
     def cross(rings, n, to):
         rings[1].arrive()
 
-        def step(r):
-            SY[at(n * R, r), :] = rings[1].total(r).astype(BF16)
+        def step(r, w):
+            SY[at(n * R, r, w), :] = rings[1].total(r, w).astype(BF16)
         rows(R, step)
         mine = pl.ds(n * R, R)
         return send(SY.at[mine, :], RY.at[mine, :], to)
@@ -330,31 +345,31 @@
         crossed.wait_recv()
         t = jnp.exp(jnp.full((1, D), ls_ref[0], F32))
 
-        def step(r):
-            g = (rings[0].total(r) + RY[at(n * R, r), :].astype(F32)) * t
-            u = unit_ref[at(0, r), :]
-            inv = inv_ref[at(0, r), :][:, 0:1]
+        def step(r, w):
+            g = (rings[0].total(r, w) + RY[at(n * R, r, w), :].astype(F32)) * t
+            u = unit_ref[at(0, r, w), :]
+            inv = inv_ref[at(0, r, w), :][:, 0:1]
             along = jnp.sum(u * g, axis=1, keepdims=True)
-            gp[at(0, r), :] = (inv * (g - u * along)).astype(BF16)
-        rows(R, step)
+            gp[at(0, r, w), :] = (inv * (g - u * along)).astype(BF16)
+        rows(R, step, 16)
 
     def feature_grad(gp, w_ref, lo):
         gf_ref[lo:lo + R, :] = lax.dot_general(
             gp[...], w_ref[...], NT, preferred_element_type=F32).astype(BF16)
 
     def far_over(ring, n, to):
-        def step(r):
-            SF[at(n * R, r), :] = ring.value(3, r).astype(BF16)
+        def step(r, w):
+            SF[at(n * R, r, w), :] = ring.value(3, r, w).astype(BF16)
         rows(R, step)
         mine = pl.ds(n * R, R)
         return send(SF.at[mine, :], RYF.at[mine, :], to)
 
     def far_sum(ring, n, over_y):
         over_y.wait_recv()
-        ring.far(lambda r: RYF[at(n * R, r), :])
+        ring.far(lambda r, w: RYF[at(n * R, r, w), :])
 
     core_send(3)
-    unit(1024, 512, 512, 512)
+    unit(1024, 512, 768, 256)
     core_send(2)
     core_wait(3)
     over_i = far_over(ring_i[1], 0, "yi")
@@ -368,12 +383,12 @@
     far_sum(ring_i[0], 0, over_i)
     core_wait(1)
     ring_i[0].near()
-    ring_t[0].near()
-    far_sum(ring_t[0], 1, over_t)
     core_wait(0)
     cross_i = cross(ring_i, 0, "yi")
+    far_sum(ring_t[0], 1, over_t)
+    ring_t[0].near()
+    cross_t = cross(ring_t, 1, "yt")
     ring_i[0].onward()
-    cross_t = cross(ring_t, 1, "yt")
     ring_t[0].onward()
     finish(ring_i, 0, cross_i, unitI, invI, gpI)
     finish(ring_t, 1, cross_t, unitT, invT, gpT)
@@ -386,63 +401,68 @@
     def columns(third):
         return slice(third * 384, third * 384 + 384)
 
-    def products(a):
-        for third in range(3):
-            accI[a * 4 * SLOT:(a + 1) * 4 * SLOT, columns(third)] = jnp.dot(
-                XP[third, a * 4 * SLOT:(a + 1) * 4 * SLOT, :], GL[:, columns(third)],
-                preferred_element_type=F32)
+    def product(third, lo, n):
+        return jnp.dot(XP[third, lo:lo + n, :], GL[:, columns(third)], preferred_element_type=F32)
 
     def weight_ring(third, axis, n, lo, stage, rx, rf, sources):
         return Ring(
-            axis, n, lo, lambda p, r: accI[at(p * n, r), columns(third)],
+            axis, n, lo, lambda p, r, w: accI[at(p * n, r, w), columns(third)],
             lambda p: stage.at[third, pl.ds(p * n, n), :],
-            lambda d: rx.at[third, d], lambda d: rf.at[third, d], sources)
-
-    outer = [weight_ring(k, AXES[k][0], 4 * SLOT, 2 * SLOT, S1, RX1, RF1, 2) for k in range(3)]
+            lambda d: rx.at[third, d], lambda d: rf.at[third, d], sources, SLOT)
+
+    N, half = 4 * SLOT, 2 * SLOT
+    outer = [weight_ring(k, AXES[k][0], N, half, S1, RX1, RF1, 2) for k in range(3)]
     inner = [weight_ring(k, AXES[k][1], SLOT, 0, S2, None, RF2, 3) for k in range(3)]
     grad_in.wait_recv()
-    products(3)
-    every(outer, "far")
-    products(1)
-    products(2)
-    every(outer, "near")
+    for third in range(3):
+        S1[third, 3 * N:4 * N, :] = product(third, 3 * N, N).astype(BF16)
+        outer[third].staged_far()
+    for third in range(3):
+        v = product(third, N, N)
+        accI[N:N + half, columns(third)] = v[:half]
+        S1[third, N + half:2 * N, :] = v[half:].astype(BF16)
+        v = product(third, 2 * N, N)
+        S1[third, 2 * N:2 * N + half, :] = v[:half].astype(BF16)
+        accI[2 * N + half:3 * N, columns(third)] = v[half:]
+        outer[third].staged_near()
     every(outer, "onward")
-    products(0)
+    for third in range(3):
+        accI[0:N, columns(third)] = product(third, 0, N)
     feature_grad(gpI, WI, 0)
     feature_grad(gpT, WT, R)
     for third in range(3):
         outer[third].arrive()
 
-        def step(r):
-            accI[at(0, r), columns(third)] = outer[third].total(r)
-        rows(4 * SLOT, step)
+        def step(r, w):
+            accI[at(0, r, w), columns(third)] = outer[third].total(r, w)
+        rows(N, step, SLOT)
         inner[third].direct()
+
     last = []
     for third in range(3):
+        c_axis = AXES[third][2]
+        row = lax.broadcasted_iota(jnp.int32, (R, SLOT), 0)
+        k = lax.broadcasted_iota(jnp.int32, (R, SLOT), 1)
+        block, i = row >> 4, row & 15
+        other = block & 1
+        core = other + me["core"] - 2 * other * me["core"]
+        want = ring_place(block >> 1, me[c_axis]) * 18 + core * 9 + i
+        pick = jnp.where((k == want) & (i < 9), 1.0, 0.0).astype(BF16)
         inner[third].arrive()
-
-        def step(r):
-            Z[third, at(0, r), :] = inner[third].total(r).astype(BF16)
-        rows(SLOT, step)
-        for k, there in enumerate("+-2"):
-            last.append(send(Z.at[third, pl.ds(0, SLOT), :],
-                             Z.at[third, pl.ds((k + 1) * SLOT, SLOT), :], AXES[third][2] + there))
+        mine = inner[third].total(0, SLOT).astype(BF16)
+        E[third] = jnp.dot(pick, mine, preferred_element_type=F32).astype(BF16)
+        for j, there in enumerate(("core", "+", "+c", "-", "-c", "2", "2c"), 1):
+            some = pl.ds(j * 16, 16)
+            last.append(send(E.at[third, some, :], Z.at[third, some, :],
+                             there if j == 1 else c_axis + there))
     for third in range(3):
-        for copy in last[third * 3:third * 3 + 3]:
+        for copy in last[third * 7:third * 7 + 7]:
             copy.wait_recv()
-        row = lax.broadcasted_iota(jnp.int32, (32, 4 * SLOT), 0)
-        k = lax.broadcasted_iota(jnp.int32, (32, 4 * SLOT), 1)
-        k = k - SLOT * over(k, SLOT)
-        theirs = (row >= 16).astype(jnp.int32)
-        i = row - 16 * theirs
-        core = theirs + me["core"] - 2 * theirs * me["core"]
-        want = me[AXES[third][2]] * 18 + core * 9 + i
-        pick = jnp.where((k == want) & (i < 9), 1.0, 0.0).astype(BF16)
-        DM[:, columns(third)] = jnp.dot(pick, Z[third], preferred_element_type=F32)
-    swap = send(DM.at[pl.ds(16, 16), :], DR, "core")
-    swap.wait_recv()
-    dw_ref[0:16, :] = jnp.where(first, DM[0:16, :], DR[...])
-    dw_ref[16:32, :] = jnp.where(first, DR[...], DM[0:16, :])
+        z = Z[third, 16:128, :].astype(F32)
+        same = E[third, 0:16, :].astype(F32) + z[16:32] + z[48:64] + z[80:96]
+        swapped = z[0:16] + z[32:48] + z[64:80] + z[96:112]
+        dw_ref[0:16, columns(third)] = jnp.where(first, same, swapped)
+        dw_ref[16:32, columns(third)] = jnp.where(first, swapped, same)
     for copy in sent:
         if copy is not feat_out:
             copy.wait_send()
@@ -458,8 +478,7 @@
              (256, BF16), (256, BF16), (256, BF16), (256, BF16), (D, BF16), (D, BF16),
              (R, BF16), (R, BF16), (R, F32), (R, F32), (R, BF16), (R, BF16),
              (2 * R, BF16), (2 * R, BF16), (R, BF16)]
-    thirds = [(4 * 4 * SLOT,), (2, 2 * SLOT), (2, 4 * SLOT), (4 * SLOT,), (3, SLOT),
-              (4 * SLOT,)]
+    thirds = [(4 * 4 * SLOT,), (2, 2 * SLOT), (2, 4 * SLOT), (4 * SLOT,), (3, SLOT), (R,), (R,)]
     return pl.pallas_call(
         kernel,
         out_shape=(jax.ShapeDtypeStruct((2 * R, D), BF16), jax.ShapeDtypeStruct((32, D), F32)),
@@ -469,7 +488,6 @@
         + [pltpu.VMEM((R, 128), F32)] * 2
         + [pltpu.VMEM((3, 16 * SLOT, 2 * R), BF16)]
         + [pltpu.VMEM((3,) + n + (D // 3,), BF16) for n in thirds]
-        + [pltpu.VMEM((32, D), F32), pltpu.VMEM((16, D), F32)]
         + [pltpu.SemaphoreType.DMA((4,))] + [pltpu.SemaphoreType.DMA((120,))] * 2,
         compiler_params=pltpu.CompilerParams(
             collective_id=0, has_side_effects=True, vmem_limit_bytes=62 * 2**20),

time: 101 us -> 97.2 us (0.962)
  Pallas kernels: 95.8 us -> 91.6 us
    pallas_call x1, Pallas kernels: 95.8 us -> 91.6 us  [fused(): pl.pallas_call(kernel, out_shape=(jax.ShapeDtypeStruct((2 * R, D), BF16),...]
where the time goes in v5:
time: 97.2 us; the launch traced here: 97 us
  Pallas kernels  91.6 us (94%)
  local copies, waits for them, and re-layouts  3.49 us (4%)
  between operations  1.93 us (2%)
    pallas_call x1, Pallas kernels, fused(): pl.pallas_call(kernel, out_shape=(jax.ShapeDtypeStruct((2 * R, D), BF16),...  91.6 us
    slice x2, local copies, waits for them, and re-layouts, body(): return (gf[:R], gf[R:], dw[0:9], dw[16:25])  3.49 us

profile of v5, /device:TPU:1, one launch (start us, length us, event | category | flops | bytes accessed | tf_op | source)
XLA Modules:
  0.0 97.0 jit_solution(272447655895288615)
XLA Ops:
  1.9 91.6 %shard_map.93 = (bf16[256,1152]{1,0:T(8,128)(2,1)}, f32[32,1152]{1,0:T(8,128)}) custom-call(bf16[128,1152]{1,0:T(8,128)(2,1)} %img_hbm.1, bf16[128,1152]{1,0:T(8,128)(2,1)} %txt_hbm.1, bf16[1152,1152]{1,0:T(8,128)(2,1)} %wi_hbm.1, bf16[1152,1152]{1,0:T(8,128)(2,1)} %wt_hbm.1, f32[1]{0:T(128)S(6)} %copy.10.ls_ref, f32[1]{0:T(128)S(6)} %copy.11.bias_ref), custom_call_target="tpu_custom_call" | custom-call | tf_op jit(solution)/shard_map/pallas_call | solution.py:482
  93.5 1.9 %fusion = (bf16[128,1152]{1,0:T(8,128)(2,1)}, bf16[128,1152]{1,0:T(8,128)(2,1)}) fusion(bf16[256,1152]{1,0:T(8,128)(2,1)} %get-tuple-element.6), kind=kLoop, calls=%fused_computation | loop fusion | bytes 1179648 | tf_op jit(solution)/shard_map/slice | solution.py:499
  95.4 1.6 %fusion.1 = (f32[9,1152]{1,0:T(8,128)}, f32[9,1152]{1,0:T(8,128)}) fusion(f32[32,1152]{1,0:T(8,128)} %get-tuple-element.7), kind=kLoop, calls=%fused_computation.1 | loop fusion | bytes 165888 | tf_op jit(solution)/shard_map/slice | solution.py:499

commit v6 on v5

--- a/solution.py
+++ b/solution.py
@@ -63,7 +63,7 @@
     D = IMG.shape[1]
     loads = [pltpu.make_async_copy(src, dst, lsem.at[k]) for k, (src, dst) in enumerate(
         ((img_hbm, IMG), (wi_hbm, WI), (txt_hbm, TXT), (wt_hbm, WT)))]
-    for load in loads:
+    for load in loads[:2]:
         load.start()
     me = place()
     near, greeted = neighbours(me)
@@ -104,17 +104,34 @@
 
     ig, tg, core_in = {}, {}, {}
 
-    def spread(got, slot, y, ring):
-        got["+", y] = send(slot(0, y), slot(2, y), ring + "+")
-        got["-", y] = send(slot(0, y), slot(1, y), ring + "-")
-
-    def near_in(got, y):
-        got["+", y].wait_recv()
-        got["-", y].wait_recv()
-
-    def onward_halves(got, slot, ring):
+    def spread(got, slot, y, ring, halves=(0, 1)):
+        for h in halves:
+            got["+", y, h] = send(slot(0, y, h * H, H), slot(2, y, h * H, H), ring + "+")
+            low = h * H if y else H - h * H
+            got["-", y, h] = send(slot(0, y, low, H), slot(1, y, low, H), ring + "-")
+
+    def to_y(got, slot, to):
+        for h in range(2):
+            got["y", h] = send(slot(0, 0, h * H, H), slot(0, 1, h * H, H), to)
+
+    def pass_on(got, slot, ring):
+        got["+", 0, 0].wait_recv()
         got["far+"] = send(slot(2, 0, 0, H), slot(3, 0, 0, H), ring + "+")
+        got["-", 0, 0].wait_recv()
         got["far-"] = send(slot(1, 0, H, H), slot(3, 0, H, H), ring + "-")
+        got["y", 0].wait_recv()
+        spread(got, slot, 1, ring, (0,))
+
+    def pass_rest(got, slot, ring):
+        got["y", 1].wait_recv()
+        spread(got, slot, 1, ring, (1,))
+        got["+", 0, 1].wait_recv()
+        got["-", 0, 1].wait_recv()
+
+    def second_in(got):
+        for d in "+-":
+            for h in range(2):
+                got[d, 1, h].wait_recv()
 
     def far_in(got, slot, to):
         got["far+"].wait_recv()
@@ -131,15 +148,17 @@
 
     loads[0].wait()
     loads[1].wait()
+    loads[2].start()
+    loads[3].start()
     project(IMG, WI, unitI, invI, I)
     pl.semaphore_wait(barrier, len(greeted))
-    ig["y"] = send(own(0, 0), own(0, 1), "yi")
+    to_y(ig, own, "yi")
     spread(ig, own, 0, "x")
     to_core((0, 0))
     loads[2].wait()
     loads[3].wait()
     project(TXT, WT, unitT, invT, T)
-    tg["y"] = send(tslot(0, 0), tslot(0, 1), "yt")
+    to_y(tg, tslot, "yt")
     spread(tg, tslot, 0, "z")
     FL[0:R, :] = jnp.where(first, IMG[...], TXT[...])
     OUT[...] = jnp.where(first, TXT[...], IMG[...])
@@ -148,7 +167,9 @@
 
     feat_out.wait_recv()
     feats = FL[...]
-    for third, (a_axis, b_axis, c_axis) in enumerate(AXES):
+    def arrange_third(third):
+        a_axis, b_axis, c_axis = AXES[third]
+
         def arrange(a, carry):
             s = lax.broadcasted_iota(jnp.int32, (4 * SLOT, 128), 0)
             b = over(s, SLOT)
@@ -167,16 +188,14 @@
             return carry
         lax.fori_loop(0, 4, arrange, 0)
 
-    near_in(ig, 0)
-    onward_halves(ig, own, "x")
-    to_core((1, 0), (2, 0))
-    near_in(tg, 0)
-    onward_halves(tg, tslot, "z")
-    ig["y"].wait_recv()
-    spread(ig, own, 1, "x")
-    to_core((0, 1))
-    tg["y"].wait_recv()
-    spread(tg, tslot, 1, "z")
+    arrange_third(0)
+    arrange_third(1)
+    pass_on(ig, own, "x")
+    pass_on(tg, tslot, "z")
+    arrange_third(2)
+    pass_rest(ig, own, "x")
+    to_core((0, 1), (1, 0), (2, 0))
+    pass_rest(tg, tslot, "z")
 
     scale = jnp.exp(jnp.full((1, 512), ls_ref[0], F32))
     slope = scale * (-LOG2E)
@@ -209,15 +228,14 @@
     far_in(tg, tslot, "yt")
     from_core((0, 0), (0, 1), (1, 0), (2, 0))
     unit(0, 1024, 0, 512, True, True, True)
-    near_in(ig, 1)
+    second_in(ig)
     to_core((1, 1), (2, 1))
-    near_in(tg, 1)
+    second_in(tg)
     unit(0, 1024, 512, 256, False, True)
     ig["far y"].wait_recv()
     to_core((3, 1))
     from_core((1, 1), (2, 1))
     unit(1024, 512, 0, 512, True)
-    unit(1024, 512, 512, 256)
     tg["far y"].wait_recv()
     from_core((3, 0), (3, 1))
     unit(1536, 512, 0, 512, True)
@@ -317,79 +335,89 @@
                 v = v + self.rf(k)[at(0, r, w), :].astype(F32)
             return v
 
-    def block_ring(axis, y, value, stage, rx, rf):
-        return Ring(
-            axis, R, H, lambda p, r, w: value(p, y, r, w),
-            lambda p: stage.at[pl.ds(ORDER[p][y] * R, R), :],
-            lambda d: rx.at[pl.ds(d * H, H), :],
-            lambda d: rf.at[pl.ds((d * 2 + y) * R, R), :])
-
-    ring_i = [block_ring("x", y, value_i, SXI, RXI, RFI) for y in range(2)]
-    ring_t = [block_ring("z", y, value_t, SXT, RXT, RFT) for y in range(2)]
+    def block_rings(axis, y, value, stage, rx, rf):
+        def half(h):
+            return Ring(
+                axis, H, H // 2, lambda p, r, w: value(p, y, h * H + r, w),
+                lambda p: stage.at[pl.ds(ORDER[p][y] * R + h * H, H), :],
+                lambda d: rx.at[pl.ds(d * H + h * (H // 2), H // 2), :],
+                lambda d: rf.at[pl.ds((d * 2 + y) * R + h * H, H), :])
+        return [half(0), half(1)]
+
+    ring_i = [block_rings("x", y, value_i, SXI, RXI, RFI) for y in range(2)]
+    ring_t = [block_rings("z", y, value_t, SXT, RXT, RFT) for y in range(2)]
 
     def every(rings, what):
         for ring in rings:
             getattr(ring, what)()
 
+    def over_y(n, h, value, stage, arrived, to):
+        lo = n * R + h * H
+
+        def step(r, w):
+            stage[at(lo, r, w), :] = value(r, w).astype(BF16)
+        rows(H, step)
+        mine = pl.ds(lo, H)
+        return send(stage.at[mine, :], arrived.at[mine, :], to)
+
+    def far_over(rings, n, to):
+        return [over_y(n, h, lambda r, w: rings[1][h].value(3, r, w), SF, RYF, to)
+                for h in range(2)]
+
+    def far_sum(rings, n, copies):
+        for h in range(2):
+            copies[h].wait_recv()
+            rings[0][h].far(lambda r, w: RYF[at(n * R + h * H, r, w), :])
+
     def cross(rings, n, to):
-        rings[1].arrive()
-
-        def step(r, w):
-            SY[at(n * R, r, w), :] = rings[1].total(r, w).astype(BF16)
-        rows(R, step)
-        mine = pl.ds(n * R, R)
-        return send(SY.at[mine, :], RY.at[mine, :], to)
+        copies = []
+        for h in range(2):
+            rings[1][h].arrive()
+            copies.append(over_y(n, h, rings[1][h].total, SY, RY, to))
+        return copies
 
     def finish(rings, n, crossed, unit_ref, inv_ref, gp):
-        rings[0].arrive()
-        crossed.wait_recv()
         t = jnp.exp(jnp.full((1, D), ls_ref[0], F32))
 
-        def step(r, w):
-            g = (rings[0].total(r, w) + RY[at(n * R, r, w), :].astype(F32)) * t
-            u = unit_ref[at(0, r, w), :]
-            inv = inv_ref[at(0, r, w), :][:, 0:1]
-            along = jnp.sum(u * g, axis=1, keepdims=True)
-            gp[at(0, r, w), :] = (inv * (g - u * along)).astype(BF16)
-        rows(R, step, 16)
+        for h in range(2):
+            rings[0][h].arrive()
+            crossed[h].wait_recv()
+
+            def step(r, w):
+                low = h * H + r
+                g = (rings[0][h].total(r, w) + RY[at(n * R, low, w), :].astype(F32)) * t
+                u = unit_ref[at(0, low, w), :]
+                inv = inv_ref[at(0, low, w), :][:, 0:1]
+                along = jnp.sum(u * g, axis=1, keepdims=True)
+                gp[at(0, low, w), :] = (inv * (g - u * along)).astype(BF16)
+            rows(H, step, 16)
 
     def feature_grad(gp, w_ref, lo):
         gf_ref[lo:lo + R, :] = lax.dot_general(
             gp[...], w_ref[...], NT, preferred_element_type=F32).astype(BF16)
 
-    def far_over(ring, n, to):
-        def step(r, w):
-            SF[at(n * R, r, w), :] = ring.value(3, r, w).astype(BF16)
-        rows(R, step)
-        mine = pl.ds(n * R, R)
-        return send(SF.at[mine, :], RYF.at[mine, :], to)
-
-    def far_sum(ring, n, over_y):
-        over_y.wait_recv()
-        ring.far(lambda r, w: RYF[at(n * R, r, w), :])
-
     core_send(3)
-    unit(1024, 512, 768, 256)
+    unit(1024, 512, 512, 512)
     core_send(2)
     core_wait(3)
-    over_i = far_over(ring_i[1], 0, "yi")
+    over_i = far_over(ring_i, 0, "yi")
     core_wait(2)
-    ring_i[1].whole()
+    every(ring_i[1], "whole")
     unit(0, 1024, 768, 256)
-    over_t = far_over(ring_t[1], 1, "yt")
+    over_t = far_over(ring_t, 1, "yt")
     core_send(1)
     core_send(0)
-    ring_t[1].whole()
-    far_sum(ring_i[0], 0, over_i)
+    every(ring_t[1], "whole")
+    far_sum(ring_i, 0, over_i)
     core_wait(1)
-    ring_i[0].near()
+    every(ring_i[0], "near")
     core_wait(0)
     cross_i = cross(ring_i, 0, "yi")
-    far_sum(ring_t[0], 1, over_t)
-    ring_t[0].near()
+    far_sum(ring_t, 1, over_t)
+    every(ring_t[0], "near")
     cross_t = cross(ring_t, 1, "yt")
-    ring_i[0].onward()
-    ring_t[0].onward()
+    every(ring_i[0], "onward")
+    every(ring_t[0], "onward")
     finish(ring_i, 0, cross_i, unitI, invI, gpI)
     finish(ring_t, 1, cross_t, unitT, invT, gpT)
 
@@ -488,7 +516,7 @@
         + [pltpu.VMEM((R, 128), F32)] * 2
         + [pltpu.VMEM((3, 16 * SLOT, 2 * R), BF16)]
         + [pltpu.VMEM((3,) + n + (D // 3,), BF16) for n in thirds]
-        + [pltpu.SemaphoreType.DMA((4,))] + [pltpu.SemaphoreType.DMA((120,))] * 2,
+        + [pltpu.SemaphoreType.DMA((4,))] + [pltpu.SemaphoreType.DMA((144,))] * 2,
         compiler_params=pltpu.CompilerParams(
             collective_id=0, has_side_effects=True, vmem_limit_bytes=62 * 2**20),
     )(img_feat, txt_feat, w_img, w_txt, ls, bias)

time: 97.2 us -> 95.2 us (0.979)
  Pallas kernels: 91.6 us -> 89.5 us
    pallas_call x1, Pallas kernels: 91.6 us -> 89.5 us  [fused(): pl.pallas_call(kernel, out_shape=(jax.ShapeDtypeStruct((2 * R, D), BF16),...]
where the time goes in v6:
time: 95.2 us; the launch traced here: 95 us
  Pallas kernels  89.5 us (94%)
  local copies, waits for them, and re-layouts  3.49 us (4%)
  between operations  1.93 us (2%)
    pallas_call x1, Pallas kernels, fused(): pl.pallas_call(kernel, out_shape=(jax.ShapeDtypeStruct((2 * R, D), BF16),...  89.5 us
    slice x2, local copies, waits for them, and re-layouts, body(): return (gf[:R], gf[R:], dw[0:9], dw[16:25])  3.49 us

profile of v6, /device:TPU:1, one launch (start us, length us, event | category | flops | bytes accessed | tf_op | source)
XLA Modules:
  0.0 95.0 jit_solution(3503868220098416322)
XLA Ops:
  1.9 89.5 %shard_map.93 = (bf16[256,1152]{1,0:T(8,128)(2,1)}, f32[32,1152]{1,0:T(8,128)}) custom-call(bf16[128,1152]{1,0:T(8,128)(2,1)} %img_hbm.1, bf16[128,1152]{1,0:T(8,128)(2,1)} %txt_hbm.1, bf16[1152,1152]{1,0:T(8,128)(2,1)} %wi_hbm.1, bf16[1152,1152]{1,0:T(8,128)(2,1)} %wt_hbm.1, f32[1]{0:T(128)S(6)} %copy.10.ls_ref, f32[1]{0:T(128)S(6)} %copy.11.bias_ref), custom_call_target="tpu_custom_call" | custom-call | tf_op jit(solution)/shard_map/pallas_call | solution.py:510
  91.5 1.9 %fusion = (bf16[128,1152]{1,0:T(8,128)(2,1)}, bf16[128,1152]{1,0:T(8,128)(2,1)}) fusion(bf16[256,1152]{1,0:T(8,128)(2,1)} %get-tuple-element.6), kind=kLoop, calls=%fused_computation | loop fusion | bytes 1179648 | tf_op jit(solution)/shard_map/slice | solution.py:527
  93.4 1.6 %fusion.1 = (f32[9,1152]{1,0:T(8,128)}, f32[9,1152]{1,0:T(8,128)}) fusion(f32[32,1152]{1,0:T(8,128)} %get-tuple-element.7), kind=kLoop, calls=%fused_computation.1 | loop fusion | bytes 165888 | tf_op jit(solution)/shard_map/slice | solution.py:527

commit v7 on v6

--- a/solution.py
+++ b/solution.py
@@ -238,8 +238,6 @@
     unit(1024, 512, 0, 512, True)
     tg["far y"].wait_recv()
     from_core((3, 0), (3, 1))
-    unit(1536, 512, 0, 512, True)
-    unit(1536, 512, 512, 512)
 
     def rows(n, step, size=32):
         def one(k, carry):
@@ -396,9 +394,13 @@
         gf_ref[lo:lo + R, :] = lax.dot_general(
             gp[...], w_ref[...], NT, preferred_element_type=F32).astype(BF16)
 
+    unit(1536, 512, 0, 512, True)
+    every(ring_t[0], "near")
+    unit(1536, 512, 512, 512)
     core_send(3)
     unit(1024, 512, 512, 512)
     core_send(2)
+    every(ring_t[1], "whole")
     core_wait(3)
     over_i = far_over(ring_i, 0, "yi")
     core_wait(2)
@@ -407,15 +409,13 @@
     over_t = far_over(ring_t, 1, "yt")
     core_send(1)
     core_send(0)
-    every(ring_t[1], "whole")
     far_sum(ring_i, 0, over_i)
     core_wait(1)
     every(ring_i[0], "near")
+    cross_t = cross(ring_t, 1, "yt")
     core_wait(0)
+    far_sum(ring_t, 1, over_t)
     cross_i = cross(ring_i, 0, "yi")
-    far_sum(ring_t, 1, over_t)
-    every(ring_t[0], "near")
-    cross_t = cross(ring_t, 1, "yt")
     every(ring_i[0], "onward")
     every(ring_t[0], "onward")
     finish(ring_i, 0, cross_i, unitI, invI, gpI)
@@ -522,9 +522,25 @@
     )(img_feat, txt_feat, w_img, w_txt, ls, bias)
 
 
+def split(gf_ref, dw_ref, gfi_ref, gft_ref, dwi_ref, dwt_ref):
+    gfi_ref[...] = gf_ref[0:R, :]
+    gft_ref[...] = gf_ref[R:2 * R, :]
+    dwi_ref[...] = dw_ref[0:9, :]
+    dwt_ref[...] = dw_ref[16:25, :]
+
+
+def outputs(gf, dw):
+    D = gf.shape[1]
+    vmem = pl.BlockSpec(memory_space=pltpu.VMEM)
+    return pl.pallas_call(
+        split,
+        out_shape=(jax.ShapeDtypeStruct((R, D), BF16),) * 2 + (jax.ShapeDtypeStruct((9, D), F32),) * 2,
+        in_specs=[vmem] * 2, out_specs=(vmem,) * 4)(gf, dw)
+
+
 def body(img_feat, txt_feat, w_img, w_txt, logit_scale_log, bias):
     gf, dw = fused(img_feat, txt_feat, w_img, w_txt, logit_scale_log, bias)
-    return gf[:R], gf[R:], dw[0:9], dw[16:25]
+    return outputs(gf, dw)
 
 
 def solution(mesh):

time: 95.2 us -> 92.1 us (0.967)
  local copies, waits for them, and re-layouts: 3.49 us -> 0 us
    slice x2 -> x0, local copies, waits for them, and re-layouts: 3.49 us -> none  [body(): return (gf[:R], gf[R:], dw[0:9], dw[16:25])]
    pallas_call x0 -> x1, Pallas kernels: none -> 1.96 us  [outputs(): pl.pallas_call(split, out_shape=(jax.ShapeDtypeStruct((R, D), BF16),) * 2...]
    pallas_call x1, Pallas kernels: 89.5 us -> 88 us  [fused(): pl.pallas_call(kernel, out_shape=(jax.ShapeDtypeStruct((2 * R, D), BF16),...]
where the time goes in v7:
time: 92.1 us; the launch traced here: 91.9 us
  Pallas kernels  89.9 us (98%)
  between operations  1.93 us (2%)
    pallas_call x1, Pallas kernels, fused(): pl.pallas_call(kernel, out_shape=(jax.ShapeDtypeStruct((2 * R, D), BF16),...  88 us
    pallas_call x1, Pallas kernels, outputs(): pl.pallas_call(split, out_shape=(jax.ShapeDtypeStruct((R, D), BF16),) * 2...  1.96 us

profile of v7, /device:TPU:1, one launch (start us, length us, event | category | flops | bytes accessed | tf_op | source)
XLA Modules:
  0.0 91.9 jit_solution(1864258499821069561)
XLA Ops:
  1.9 88.0 %shard_map.93 = (bf16[256,1152]{1,0:T(8,128)(2,1)}, f32[32,1152]{1,0:T(8,128)}) custom-call(bf16[128,1152]{1,0:T(8,128)(2,1)} %img_hbm.1, bf16[128,1152]{1,0:T(8,128)(2,1)} %txt_hbm.1, bf16[1152,1152]{1,0:T(8,128)(2,1)} %wi_hbm.1, bf16[1152,1152]{1,0:T(8,128)(2,1)} %wt_hbm.1, f32[1]{0:T(128)S(6)} %copy.10.ls_ref, f32[1]{0:T(128)S(6)} %copy.11.bias_ref), custom_call_target="tpu_custom_call" | custom-call | tf_op jit(solution)/shard_map/pallas_call | solution.py:510
  89.9 2.0 %shard_map.94 = (bf16[128,1152]{1,0:T(8,128)(2,1)}, bf16[128,1152]{1,0:T(8,128)(2,1)}, f32[9,1152]{1,0:T(8,128)}, f32[9,1152]{1,0:T(8,128)}) custom-call(bf16[256,1152]{1,0:T(8,128)(2,1)} %get-tuple-element.6.gf_ref, f32[32,1152]{1,0:T(8,128)} %get-tuple-element.7.dw_ref), custom_call_target="tpu_custom_call" | custom-call | tf_op jit(solution)/shard_map/pallas_call | solution.py:535

commit v8 on v7

--- a/solution.py
+++ b/solution.py
@@ -58,12 +58,15 @@
 def kernel(img_hbm, txt_hbm, wi_hbm, wt_hbm, ls_ref, bias_ref,
            gf_ref, dw_ref,
            I, T, accI, accT, SC, RC, SXI, SXT, RXI, RXT, RFI, RFT, SY, RY, SF, RYF, WI, WT, IMG, TXT,
-           unitI, unitT, gpI, gpT, FL, GL, OUT, invI, invT,
+           unitI, unitT, gpI, gpT, FL, GL, GI, GT, OUT, invI, invT,
            XP, S1, RX1, RF1, S2, RF2, E, Z, lsem, ssem, rsem):
     D = IMG.shape[1]
+    K0 = 512
     loads = [pltpu.make_async_copy(src, dst, lsem.at[k]) for k, (src, dst) in enumerate(
-        ((img_hbm, IMG), (wi_hbm, WI), (txt_hbm, TXT), (wt_hbm, WT)))]
-    for load in loads[:2]:
+        ((img_hbm, IMG), (wi_hbm.at[pl.ds(0, K0), :], WI.at[pl.ds(0, K0), :]),
+         (wi_hbm.at[pl.ds(K0, D - K0), :], WI.at[pl.ds(K0, D - K0), :]),
+         (txt_hbm, TXT), (wt_hbm, WT)))]
+    for load in loads[:3]:
         load.start()
     me = place()
     near, greeted = neighbours(me)
@@ -83,8 +86,13 @@
         sent.append(copy)
         return copy
 
-    def project(feat, w, unit, inv, emb):
-        p = jnp.dot(feat[...], w[...], preferred_element_type=F32)
+    def project(feat, w, unit, inv, emb, ready):
+        ready[0].wait()
+        ready[1].wait()
+        p = jnp.dot(feat[:, :K0], w[:K0, :], preferred_element_type=F32)
+        for load in ready[2:]:
+            load.wait()
+        p = p + jnp.dot(feat[:, K0:], w[K0:, :], preferred_element_type=F32)
         r = lax.rsqrt(jnp.sum(p * p, axis=1, keepdims=True) + 1e-06)
         u = p * r
         unit[...] = u
@@ -146,18 +154,14 @@
         for place_y in places:
             core_in[place_y].wait_recv()
 
-    loads[0].wait()
-    loads[1].wait()
-    loads[2].start()
     loads[3].start()
-    project(IMG, WI, unitI, invI, I)
+    loads[4].start()
+    project(IMG, WI, unitI, invI, I, loads[:3])
     pl.semaphore_wait(barrier, len(greeted))
     to_y(ig, own, "yi")
     spread(ig, own, 0, "x")
     to_core((0, 0))
-    loads[2].wait()
-    loads[3].wait()
-    project(TXT, WT, unitT, invT, T)
+    project(TXT, WT, unitT, invT, T, loads[3:])
     to_y(tg, tslot, "yt")
     spread(tg, tslot, 0, "z")
     FL[0:R, :] = jnp.where(first, IMG[...], TXT[...])
@@ -239,7 +243,7 @@
     tg["far y"].wait_recv()
     from_core((3, 0), (3, 1))
 
-    def rows(n, step, size=32):
+    def rows(n, step, size=64):
         def one(k, carry):
             step(k * size, size)
             return carry
@@ -302,10 +306,6 @@
             self.piece("a+", 1, 0, self.n, "+", self.rf(0), 0)
             self.piece("a-", 2, 0, self.n, "-", self.rf(1), 0)
 
-        def direct(self):
-            for k, (p, there) in enumerate(((3, "2"), (1, "+"), (2, "-"))):
-                self.piece(there, p, 0, self.n, there, self.rf(k), 0)
-
         def onward(self):
             lo, hi = self.lo, self.n - self.lo
             self.got["far+"].wait_recv()
@@ -388,7 +388,7 @@
                 inv = inv_ref[at(0, low, w), :][:, 0:1]
                 along = jnp.sum(u * g, axis=1, keepdims=True)
                 gp[at(0, low, w), :] = (inv * (g - u * along)).astype(BF16)
-            rows(H, step, 16)
+            rows(H, step, 32)
 
     def feature_grad(gp, w_ref, lo):
         gf_ref[lo:lo + R, :] = lax.dot_general(
@@ -419,12 +419,12 @@
     every(ring_i[0], "onward")
     every(ring_t[0], "onward")
     finish(ring_i, 0, cross_i, unitI, invI, gpI)
+    GI[0:R, :] = gpI[...]
+    grad_i = send(gpI, GI.at[pl.ds(R, R), :], "core")
     finish(ring_t, 1, cross_t, unitT, invT, gpT)
 
-    GL[0:R, :] = jnp.where(first, gpI[...], gpT[...])
-    feat_out.wait_send()
-    OUT[...] = jnp.where(first, gpT[...], gpI[...])
-    grad_in = send(OUT, GL.at[pl.ds(R, R), :], "core")
+    grad_t = send(gpT, GT.at[pl.ds(R, R), :], "core")
+    GT[0:R, :] = gpT[...]
 
     def columns(third):
         return slice(third * 384, third * 384 + 384)
@@ -441,7 +441,10 @@
     N, half = 4 * SLOT, 2 * SLOT
     outer = [weight_ring(k, AXES[k][0], N, half, S1, RX1, RF1, 2) for k in range(3)]
     inner = [weight_ring(k, AXES[k][1], SLOT, 0, S2, None, RF2, 3) for k in range(3)]
-    grad_in.wait_recv()
+    feature_grad(gpI, WI, 0)
+    grad_i.wait_recv()
+    grad_t.wait_recv()
+    GL[...] = jnp.where(first, GI[...], GT[...])
     for third in range(3):
         S1[third, 3 * N:4 * N, :] = product(third, 3 * N, N).astype(BF16)
         outer[third].staged_far()
@@ -456,15 +459,14 @@
     every(outer, "onward")
     for third in range(3):
         accI[0:N, columns(third)] = product(third, 0, N)
-    feature_grad(gpI, WI, 0)
     feature_grad(gpT, WT, R)
     for third in range(3):
         outer[third].arrive()
 
-        def step(r, w):
-            accI[at(0, r, w), columns(third)] = outer[third].total(r, w)
-        rows(N, step, SLOT)
-        inner[third].direct()
+        for k, (p, there) in enumerate(((3, "2"), (1, "+"), (2, "-"))):
+            S2[third, p * SLOT:(p + 1) * SLOT, :] = outer[third].total(p * SLOT, SLOT).astype(BF16)
+            inner[third].launch(there, p, 0, SLOT, there, inner[third].rf(k), 0)
+        accI[0:SLOT, columns(third)] = outer[third].total(0, SLOT)
 
     last = []
     for third in range(3):
@@ -492,8 +494,7 @@
         dw_ref[0:16, columns(third)] = jnp.where(first, same, swapped)
         dw_ref[16:32, columns(third)] = jnp.where(first, swapped, same)
     for copy in sent:
-        if copy is not feat_out:
-            copy.wait_send()
+        copy.wait_send()
 
 
 def fused(img_feat, txt_feat, w_img, w_txt, ls, bias):
@@ -505,7 +506,7 @@
              (1024, BF16), (1024, BF16), (R, BF16), (R, BF16), (512, BF16), (512, BF16),
              (256, BF16), (256, BF16), (256, BF16), (256, BF16), (D, BF16), (D, BF16),
              (R, BF16), (R, BF16), (R, F32), (R, F32), (R, BF16), (R, BF16),
-             (2 * R, BF16), (2 * R, BF16), (R, BF16)]
+             (2 * R, BF16), (2 * R, BF16), (2 * R, BF16), (2 * R, BF16), (R, BF16)]
     thirds = [(4 * 4 * SLOT,), (2, 2 * SLOT), (2, 4 * SLOT), (4 * SLOT,), (3, SLOT), (R,), (R,)]
     return pl.pallas_call(
         kernel,
@@ -516,7 +517,7 @@
         + [pltpu.VMEM((R, 128), F32)] * 2
         + [pltpu.VMEM((3, 16 * SLOT, 2 * R), BF16)]
         + [pltpu.VMEM((3,) + n + (D // 3,), BF16) for n in thirds]
-        + [pltpu.SemaphoreType.DMA((4,))] + [pltpu.SemaphoreType.DMA((144,))] * 2,
+        + [pltpu.SemaphoreType.DMA((5,))] + [pltpu.SemaphoreType.DMA((144,))] * 2,
         compiler_params=pltpu.CompilerParams(
             collective_id=0, has_side_effects=True, vmem_limit_bytes=62 * 2**20),
     )(img_feat, txt_feat, w_img, w_txt, ls, bias)

time: 92.1 us -> 91.1 us (0.989)
  no operation moved by 1% of the time
where the time goes in v8:
time: 91.1 us; the launch traced here: 91 us
  Pallas kernels  89.1 us (98%)
  between operations  1.93 us (2%)
    pallas_call x1, Pallas kernels, fused(): pl.pallas_call(kernel, out_shape=(jax.ShapeDtypeStruct((2 * R, D), BF16),...  87.1 us
    pallas_call x1, Pallas kernels, outputs(): pl.pallas_call(split, out_shape=(jax.ShapeDtypeStruct((R, D), BF16),) * 2...  1.96 us

profile of v8, /device:TPU:1, one launch (start us, length us, event | category | flops | bytes accessed | tf_op | source)
XLA Modules:
  0.0 91.0 jit_solution(16555486839011807411)
XLA Ops:
  1.9 87.1 %shard_map.93 = (bf16[256,1152]{1,0:T(8,128)(2,1)}, f32[32,1152]{1,0:T(8,128)}) custom-call(bf16[128,1152]{1,0:T(8,128)(2,1)} %img_hbm.1, bf16[128,1152]{1,0:T(8,128)(2,1)} %txt_hbm.1, bf16[1152,1152]{1,0:T(8,128)(2,1)} %wi_hbm.1, bf16[1152,1152]{1,0:T(8,128)(2,1)} %wt_hbm.1, f32[1]{0:T(128)S(6)} %copy.10.ls_ref, f32[1]{0:T(128)S(6)} %copy.11.bias_ref), custom_call_target="tpu_custom_call" | custom-call | tf_op jit(solution)/shard_map/pallas_call | solution.py:511
  89.0 2.0 %shard_map.94 = (bf16[128,1152]{1,0:T(8,128)(2,1)}, bf16[128,1152]{1,0:T(8,128)(2,1)}, f32[9,1152]{1,0:T(8,128)}, f32[9,1152]{1,0:T(8,128)}) custom-call(bf16[256,1152]{1,0:T(8,128)(2,1)} %get-tuple-element.6.gf_ref, f32[32,1152]{1,0:T(8,128)} %get-tuple-element.7.dw_ref), custom_call_target="tpu_custom_call" | custom-call | tf_op jit(solution)/shard_map/pallas_call | solution.py:536

commit v9 on v8

--- a/solution.py
+++ b/solution.py
@@ -86,12 +86,14 @@
         sent.append(copy)
         return copy
 
-    def project(feat, w, unit, inv, emb, ready):
+    def project(feat, w, unit, inv, emb, ready, following=()):
         ready[0].wait()
         ready[1].wait()
         p = jnp.dot(feat[:, :K0], w[:K0, :], preferred_element_type=F32)
         for load in ready[2:]:
             load.wait()
+        for load in following:
+            load.start()
         p = p + jnp.dot(feat[:, K0:], w[K0:, :], preferred_element_type=F32)
         r = lax.rsqrt(jnp.sum(p * p, axis=1, keepdims=True) + 1e-06)
         u = p * r
@@ -154,9 +156,7 @@
         for place_y in places:
             core_in[place_y].wait_recv()
 
-    loads[3].start()
-    loads[4].start()
-    project(IMG, WI, unitI, invI, I, loads[:3])
+    project(IMG, WI, unitI, invI, I, loads[:3], loads[3:])
     pl.semaphore_wait(barrier, len(greeted))
     to_y(ig, own, "yi")
     spread(ig, own, 0, "x")

time: 91.1 us -> 91.3 us (level)
  no operation moved by 1% of the time
where the time goes in v9:
time: 91.3 us; the launch traced here: 91.1 us
  Pallas kernels  89.2 us (98%)
  between operations  1.93 us (2%)
    pallas_call x1, Pallas kernels, fused(): pl.pallas_call(kernel, out_shape=(jax.ShapeDtypeStruct((2 * R, D), BF16),...  87.2 us
    pallas_call x1, Pallas kernels, outputs(): pl.pallas_call(split, out_shape=(jax.ShapeDtypeStruct((R, D), BF16),) * 2...  1.96 us

profile of v9, /device:TPU:1, one launch (start us, length us, event | category | flops | bytes accessed | tf_op | source)
XLA Modules:
  0.0 91.1 jit_solution(6739727537245417176)
XLA Ops:
  1.9 87.2 %shard_map.93 = (bf16[256,1152]{1,0:T(8,128)(2,1)}, f32[32,1152]{1,0:T(8,128)}) custom-call(bf16[128,1152]{1,0:T(8,128)(2,1)} %img_hbm.1, bf16[128,1152]{1,0:T(8,128)(2,1)} %txt_hbm.1, bf16[1152,1152]{1,0:T(8,128)(2,1)} %wi_hbm.1, bf16[1152,1152]{1,0:T(8,128)(2,1)} %wt_hbm.1, f32[1]{0:T(128)S(6)} %copy.10.ls_ref, f32[1]{0:T(128)S(6)} %copy.11.bias_ref), custom_call_target="tpu_custom_call" | custom-call | tf_op jit(solution)/shard_map/pallas_call | solution.py:511
  89.2 2.0 %shard_map.94 = (bf16[128,1152]{1,0:T(8,128)(2,1)}, bf16[128,1152]{1,0:T(8,128)(2,1)}, f32[9,1152]{1,0:T(8,128)}, f32[9,1152]{1,0:T(8,128)}) custom-call(bf16[256,1152]{1,0:T(8,128)(2,1)} %get-tuple-element.6.gf_ref, f32[32,1152]{1,0:T(8,128)} %get-tuple-element.7.dw_ref), custom_call_target="tpu_custom_call" | custom-call | tf_op jit(solution)/shard_map/pallas_call | solution.py:536
